TPU v7x, 512 devices: a whole 4x4x16 slice. The times are simulated.
512 devices in a mesh: dp: 64 (over x, z), tensor: 8 (over y, core).
Axes of the slice: x: 4, y: 4, z: 16, core: 2. Of those that a mesh axis runs over, the one named last changes fastest.
Arguments:
- ctx: bfloat16 [16384, 5120], P('dp', 'tensor'), may hold values from -16 to 16
- resid: bfloat16 [16384, 5120], P('dp', 'tensor'), may hold values from -6 to 6
- output_projection_weight: bfloat16 [5120, 5120], P('tensor', 'dp'), may hold values from -0.078125 to 0.078125
- adapter_down_weight: bfloat16 [5120, 64], P('tensor'), may hold values from -0.078125 to 0.078125
- adapter_up_weight: bfloat16 [64, 5120], P(None, 'tensor'), may hold values from -0.75 to 0.75
- down_direction: bfloat16 [5120, 64], P('tensor'), may hold values from -0.078125 to 0.078125
- up_direction: bfloat16 [64, 5120], P(None, 'tensor'), may hold values from -0.75 to 0.75
- layer_norm_gain: float32 [5120], P('tensor'), may hold values from 0.25 to 1.75
- lengths: int32 [128], P('dp'), may hold values from 1 to 128, as said below
Outputs:
- hvp_a: float32 [5120, 64], P(('tensor', 'dp'))
- hvp_b: float32 [64, 5120], P('dp', 'tensor')
Inputs may be any that keep to these rules, and one draw needn't show every extreme that they name: `lengths`: some sequence is full in every draw.
All inputs are finite; a program needn't handle non-finite values.
Results may differ from a plain program's by a relative error of at most 0.0008.
Values may be sent and summed in bfloat16 or wider, within the bound.
A program may use at most 64 MiB of HBM per device.

v0:
```python
import jax
import jax.numpy as jnp
from jax import lax
from jax.sharding import PartitionSpec as P

SEQ_LEN = 128


def body(
    ctx,
    resid,
    output_projection_weight,
    adapter_down_weight,
    adapter_up_weight,
    down_direction,
    up_direction,
    layer_norm_gain,
    lengths,
):
    high = lax.Precision.HIGHEST
    tokens = ctx.shape[0]
    width = resid.shape[1]
    total = width * lax.axis_size("tensor")
    scale = 1.0 / jnp.sqrt(jnp.float32(tokens * lax.axis_size("dp")))
    seq_count = lengths.shape[0]
    partial_sum = jnp.dot(
        ctx,
        lax.all_gather(output_projection_weight, "dp", axis=1, tiled=True),
        preferred_element_type=jnp.float32,
    )
    lowered_value = jnp.dot(ctx, adapter_down_weight, preferred_element_type=jnp.float32)
    down_tangent = jnp.dot(ctx, down_direction, preferred_element_type=jnp.float32)
    attn = lax.psum_scatter(
        partial_sum.astype(jnp.bfloat16), "tensor", scatter_dimension=1, tiled=True
    ).astype(jnp.float32)
    reduced_rank_output, low_tangent = lax.psum((lowered_value, down_tangent), "tensor")
    raised_output = adapter_up_weight.astype(jnp.float32)
    up_tangent = up_direction.astype(jnp.float32)
    hidden = (
        attn
        + jnp.dot(reduced_rank_output, raised_output, precision=high)
        + resid.astype(jnp.float32)
    )
    tangent = jnp.dot(low_tangent, raised_output, precision=high) + jnp.dot(
        reduced_rank_output, up_tangent, precision=high
    )
    sum_h, sum_hh = lax.psum(
        (jnp.sum(hidden, axis=1, keepdims=True), jnp.sum(hidden * hidden, axis=1, keepdims=True)),
        "tensor",
    )
    center = sum_h / total
    inverse = lax.rsqrt(sum_hh / total - center * center + 1e-05)
    normed = (hidden - center) * inverse
    sum_t, sum_nt = lax.psum(
        (jnp.sum(tangent, axis=1, keepdims=True), jnp.sum(normed * tangent, axis=1, keepdims=True)),
        "tensor",
    )
    mean_t = sum_t / total
    mean_nt = sum_nt / total
    tangent_n = inverse * (tangent - mean_t - normed * mean_nt)
    limit = jnp.broadcast_to(lengths[:, None], (seq_count, SEQ_LEN)).reshape(-1)
    position = jnp.arange(tokens, dtype=jnp.int32) % SEQ_LEN
    live = (position < limit).astype(jnp.float32) * scale
    cotangent = live[:, None] * (layer_norm_gain * layer_norm_gain)[None, :] * tangent_n
    sum_c, sum_nc = lax.psum(
        (
            jnp.sum(cotangent, axis=1, keepdims=True),
            jnp.sum(normed * cotangent, axis=1, keepdims=True),
        ),
        "tensor",
    )
    grad_h = inverse * (cotangent - sum_c / total - normed * (sum_nc / total))
    part_b = jnp.dot(reduced_rank_output.T, grad_h, precision=high)
    projected = lax.psum(jnp.dot(grad_h, raised_output.T, precision=high), "tensor")
    part_a = jnp.dot(ctx.astype(jnp.float32).T, projected, precision=high)
    hvp_a, hvp_b = (
        lax.psum_scatter(part_a, "dp", scatter_dimension=0, tiled=True),
        lax.psum_scatter(part_b, "dp", scatter_dimension=0, tiled=True),
    )
    return (hvp_a, hvp_b)


def solution(mesh):
    in_specs = (
        P("dp", "tensor"),
        P("dp", "tensor"),
        P("tensor", "dp"),
        P("tensor", None),
        P(None, "tensor"),
        P("tensor", None),
        P(None, "tensor"),
        P("tensor"),
        P("dp"),
    )
    out_specs = (P(("tensor", "dp"), None), P("dp", "tensor"))
    return jax.shard_map(body, mesh=mesh, in_specs=in_specs, out_specs=out_specs, check_vma=False)
```

profile of v0, /device:TPU:1, one launch (start us, length us, event | category | flops | bytes accessed | tf_op | source)
XLA Modules:
  0.0 596.1 jit_solution(12588004231649991924)
XLA Ops:
  8.1 0.7 all-gather.2.cloned.1.call-update
  9.0 1.7 fusion.3
  10.7 1.7 fusion.4
  12.6 149.3 %all-gather.2.cloned.1.call-done = bf16[640,5120]{0,1:T(8,128)(2,1)} async-done(((bf16[640,80]{0,1:T(8,128)(2,1)}), bf16[640,5120]{0,1:T(8,128)(2,1)}) %all-gather.2.cloned.1.call-update) | async-done | bytes 6553616 | tf_op jit(solution)/shard_map/all_gather | solution.py:28
  161.9 5.1 convolution_convert_fusion
  167.0 2.6 copy.14
  169.8 1.3 fusion.5
  171.1 41.7 %reduce-scatter.5.cloned.1.call-done = bf16[640,256]{1,0:T(8,128)(2,1)} async-done(((bf16[5120,256]{1,0:T(8,128)(2,1)}), bf16[640,256]{1,0:T(8,128)(2,1)}) %reduce-scatter.5.cloned.1.call-update) | async-done | bytes 327696
  212.8 1.2 copy.15
  214.0 1.5 multiply_reduce_fusion.2
  215.5 14.3 %all-reduce.5 = (f32[256,1]{0,1:T(1,128)S(1)}, f32[256,1]{0,1:T(1,128)S(1)}) all-reduce(f32[256,1]{0,1:T(1,128)S(1)} %bitcast.55, f32[256,1]{0,1:T(1,128)S(1)} %bitcast.56), channel_id=1, replica_groups=mesh['dp'=64,'tensor'=8] {'tensor'}, use_global_device_ids=true, to_apply=%region_3.0 | all-reduce | flops 512 | bytes 4096 | tf_op jit(solution)/shard_map/psum | solution.py:47
  229.8 1.5 fusion.2
  231.4 13.9 %all-reduce.4 = (f32[256,1]{0,1:T(1,128)S(1)}, f32[256,1]{0,1:T(1,128)S(1)}) all-reduce(f32[256,1]{0,1:T(1,128)S(1)} %bitcast.52, f32[256,1]{0,1:T(1,128)S(1)} %bitcast.51), channel_id=1, replica_groups=mesh['dp'=64,'tensor'=8] {'tensor'}, use_global_device_ids=true, to_apply=%region_10.0 | all-reduce | flops 512 | bytes 4096 | tf_op jit(solution)/shard_map/psum | solution.py:54
  245.2 0.4 fusion.1
  245.6 12.4 %all-reduce.3 = (f32[256,1]{0,1:T(1,128)S(1)}, f32[256,1]{0,1:T(1,128)S(1)}) all-reduce(f32[256,1]{0,1:T(1,128)S(1)} %bitcast.48, f32[256,1]{0,1:T(1,128)S(1)} %bitcast.47), channel_id=1, replica_groups=mesh['dp'=64,'tensor'=8] {'tensor'}, use_global_device_ids=true, to_apply=%region_14.15 | all-reduce | flops 512 | bytes 4096 | tf_op jit(solution)/shard_map/psum | solution.py:65
  258.3 1.1 fusion.6
  259.5 1.1 fusion.7
  260.6 69.4 %all-reduce.11.cloned.1.call-done = f32[256,64]{0,1:T(8,128)} async-done(((f32[256,64]{0,1:T(8,128)}), f32[256,64]{0,1:T(8,128)}) %all-reduce.11.cloned.1.call-update) | async-done | bytes 65552 | tf_op jit(solution)/shard_map/psum | solution.py:74
  330.0 1.8 convolution_bitcast_fusion
  331.8 1.3 dynamic-slice
  333.8 251.3 %all-reduce.13.cloned.1.call-done = (f32[640,64]{0,1:T(8,128)}, f32[64,640]{1,0:T(8,128)}) async-done(((f32[640,64]{0,1:T(8,128)}, f32[64,640]{1,0:T(8,128)}), (f32[640,64]{0,1:T(8,128)}, f32[64,640]{1,0:T(8,128)})) %all-reduce.13.cloned.1.call-update) | async-done | bytes 327696
  585.0 0.9 constant_dynamic-slice_fusion.1
  586.0 0.7 copy.13
  586.6 1.9 constant_dynamic-slice_fusion
  (31 shorter events, 0.8 us)
Async XLA Ops:
  8.0 1.0 copy-start
  8.0 153.9 %all-gather.2.cloned.1.call-start = ((), (), s32[]{:S(2)}) async-start(), calls=%async_computation.1 | async-start | bytes 6656000 | tf_op jit(solution)/shard_map/all_gather | solution.py:28
  8.7 161.0 %all-reduce.15.cloned.1.call-start = ((), (), s32[]{:S(2)}) async-start(), calls=%async_computation.5 | async-start | bytes 262144 | tf_op jit(solution)/shard_map/psum | solution.py:36
  12.5 157.2 %copy-start.5 = (f32[640]{0:T(1024)S(1)}, f32[640]{0:T(1024)}, u32[]{:S(2)}) copy-start(f32[640]{0:T(1024)} %param.16) | copy-start | bytes 7684
  12.5 157.2 %copy-start.6 = (s32[2]{0:T(128)S(1)}, s32[2]{0:T(128)}, u32[]{:S(2)}) copy-start(s32[2]{0:T(128)} %param.17) | copy-start | bytes 28
  12.5 157.3 %copy-start.1 = (bf16[64,640]{1,0:T(8,128)(2,1)S(1)}, bf16[64,640]{1,0:T(8,128)(2,1)}, u32[]{:S(2)}) copy-start(bf16[64,640]{1,0:T(8,128)(2,1)} %param.13) | copy-start | bytes 245764
  12.5 200.3 %reduce-scatter.5.cloned.1.call-start = ((), (), s32[]{:S(2)}) async-start(), calls=%async_computation.3 | async-start | bytes 2949120
  167.0 47.0 %copy-start.3 = (bf16[256,640]{1,0:T(8,128)(2,1)S(1)}, bf16[256,640]{1,0:T(8,128)(2,1)}, u32[]{:S(2)}) copy-start(bf16[256,640]{1,0:T(8,128)(2,1)} %param.10) | copy-start | bytes 983044
  167.0 62.8 %copy-start.4 = (bf16[64,640]{1,0:T(8,128)(2,1)S(1)}, bf16[64,640]{1,0:T(8,128)(2,1)}, u32[]{:S(2)}) copy-start(bf16[64,640]{1,0:T(8,128)(2,1)} %param.15) | copy-start | bytes 245764
  169.6 160.4 %all-reduce.11.cloned.1.call-start = ((), (), s32[]{:S(2)}) async-start(), calls=%async_computation.2 | async-start | bytes 131072 | tf_op jit(solution)/shard_map/psum | solution.py:74
  169.8 89.7 %copy-start.2 = (f32[256,64]{0,1:T(8,128)S(1)}, f32[256,64]{0,1:T(8,128)}, u32[]{:S(2)}) copy-start(f32[256,64]{0,1:T(8,128)} %get-tuple-element.23) | copy-start | bytes 196612
  259.4 325.6 %all-reduce.13.cloned.1.call-start = ((), (), s32[]{:S(2)}) async-start(), calls=%async_computation.4 | async-start | bytes 655360
Sparse Core Ops, SparseCore 0:
  11.8 150.0 all-gather.1
  332.0 253.0 all-reduce.12
Sparse Core Ops, SparseCore 1:
  12.6 79.0 all-reduce.14
  169.7 43.0 reduce-scatter.4
  259.5 70.5 all-reduce.10
where the time goes:
time: 606 us; the launch traced here: 596 us
  waiting for transfers between devices  512 us (84%)
  blocking collectives  40.6 us (7%)
  matrix products  17 us (3%)
  between operations  16.4 us (3%)
  local copies, waits for them, and re-layouts  8.78 us (1%)
    unnamed x7, waiting for transfers between devices  294 us
    all_gather x1, waiting for transfers between devices, body(): lax.all_gather(output_projection_weight, 'dp', axis=1, tiled=True)  149 us
    psum x1, waiting for transfers between devices, body(): lax.psum(jnp.dot(grad_h, raised_output.T, precision=high), 'tensor')  69.4 us
    psum x1, blocking collectives, body(): lax.psum((jnp.sum(hidden, axis=1, keepdims=True), jnp.sum(hidden * hidden...  14.3 us
    psum x1, blocking collectives, body(): lax.psum((jnp.sum(tangent, axis=1, keepdims=True), jnp.sum(normed * tange...  13.9 us
    psum x1, blocking collectives, body(): lax.psum((jnp.sum(cotangent, axis=1, keepdims=True), jnp.sum(normed * cot...  12.4 us
  transfers between devices with their start and end apart: 5, of which 4 were waited for; matrix products, arithmetic and copies ran while one was open for 3% of the time, Pallas kernels for 0%

commit v1 on v0

v1 whole, which is shorter than its diff:
```python
import functools

import jax
import jax.numpy as jnp
from jax import lax
from jax.experimental import pallas as pl
from jax.experimental.pallas import tpu as pltpu
from jax.sharding import Mesh, PartitionSpec as P

AXES = ("x", "z", "y", "c")
NX, NZ, NY, NC = 4, 16, 4, 2
SEQ = 128
RANK = 64
FEATS = 1280
HALF = 640
COLS = 80
TOKENS = 16384
WIDTH = 5120
BF = jnp.bfloat16
F32 = jnp.float32
CHUNKS = ((0, 7), (7, 9), (9, 11), (11, 13), (13, 15), (15, 16))
NCH = len(CHUNKS)
NT = (((1,), (1,)), ((), ()))
TN = (((0,), (0,)), ((), ()))


def split2(v):
    hi = v.astype(BF)
    lo = (v - hi.astype(F32)).astype(BF)
    return hi, lo


def split3(v):
    hi = v.astype(BF)
    rest = v - hi.astype(F32)
    mid = rest.astype(BF)
    lo = (rest - mid.astype(F32)).astype(BF)
    return hi, mid, lo


def dot(a, b, dims=(((1,), (0,)), ((), ()))):
    return lax.dot_general(a, b, dims, preferred_element_type=F32)


def kernel(
    ctx_ref, resid_ref, wt_ref, at_ref, dt_ref, b_ref, u_ref, g_ref, len_ref,
    out_a, out_b,
    ctxg, wg, adg, rt, rrecv, buT, gr, part, rsb, zpart, zb, h_ref, dh_ref, gh_ref,
    st_snd, st_rcv, qg, ha_snd, ha_rcv, hb_snd, hb_rcv, ha_sum, hb_sum, buf2, rcv2,
    s_ctx, r_ctx, s_w, r_w, s_ws, r_ws, s_ad, r_ad, s_res, r_res, s_bu, r_bu, s_rs, r_rs,
    s_z, r_z, s_st, r_st, s_q, r_q, s_ha, r_ha, s_hb, r_hb, s_2, r_2,
):
    x, z, y, c = [lax.axis_index(a) for a in AXES]

    def dev(dx=0, dz=0, dy=0, dc=0):
        return (lax.rem(x + dx + NX, NX), lax.rem(z + dz + NZ, NZ), lax.rem(y + dy + NY, NY), lax.rem(c + dc, NC))

    def rcopy(src, dst, ss, rs, to):
        return pltpu.make_async_remote_copy(
            src_ref=src, dst_ref=dst, send_sem=ss, recv_sem=rs, device_id=to, device_id_type=pl.DeviceIdType.MESH
        )

    barrier = pltpu.get_barrier_semaphore()
    count = 0
    for dx in range(NX):
        for dy in range(NY):
            for dc in range(NC):
                if (dx, dy, dc) != (0, 0, 0):
                    pl.semaphore_signal(barrier, inc=1, device_id=dev(dx, 0, dy, dc), device_id_type=pl.DeviceIdType.MESH)
                    count += 1
    for dz in range(1, NZ):
        pl.semaphore_signal(barrier, inc=1, device_id=dev(0, dz), device_id_type=pl.DeviceIdType.MESH)
        count += 1
    pl.semaphore_wait(barrier, count)

    pending = []
    diag = x == y

    wr = {}

    def w_start(s, flow, src, lanes=None):
        slot = 15 if s == 8 else (2 * s - 1 if flow == 0 else 2 * s)
        dst = wg.at[c, slot]
        if s == 8:
            lanes = pl.ds(0, 384) if flow == 0 else pl.ds(384, 256)
            src, dst = src.at[:, lanes], dst.at[:, lanes]
        k = 2 * (s - 1) + flow
        cp = rcopy(src, dst, s_w.at[k], r_w.at[k], dev(0, 1 if flow == 0 else -1))
        cp.start()
        wr[(s, flow)] = cp
        pending.append(cp)

    def w_sib(slot, src):
        cp = rcopy(src, wg.at[c, slot], s_ws.at[slot], r_ws.at[slot], dev(0, 0, 0, 1))
        cp.start()
        pending.append(cp)
        return cp

    w_start(1, 0, wt_ref)
    w_start(1, 1, wt_ref)
    ctx_cp = {}
    for half in range(2):
        src = ctx_ref.at[pl.ds(half * SEQ, SEQ), :]
        for k, dx in ((1, 1), (3, -1)):
            i = (0 if dx == 1 else 2) + half
            to = (lax.rem(x + dx + NX, NX), z, y, half)
            cp = rcopy(src, ctxg.at[x, c], s_ctx.at[i], r_ctx.at[k + c], to)
            cp.start()
            pending.append(cp)
    sib_half = lax.rem(c + 1, 2)
    cp = rcopy(ctx_ref.at[pl.ds(pl.multiple_of(sib_half * SEQ, SEQ), SEQ), :], ctxg.at[x, c], s_ctx.at[4], r_ctx.at[0], dev(0, 0, 0, 1))
    cp.start()
    pending.append(cp)
    sib = [w_sib(0, wt_ref)]
    adg[c, 0:RANK] = at_ref[...]
    adg[c, RANK:] = dt_ref[...]
    ad_cp = rcopy(adg.at[c], adg.at[c], s_ad.at[0], r_ad.at[0], dev(0, 0, 0, 1))
    ad_cp.start()
    pending.append(ad_cp)
    wg[c, 0] = wt_ref[...]
    ctxg[x, c] = ctx_ref[pl.ds(pl.multiple_of(c * SEQ, SEQ), SEQ), :]

    lane = lax.broadcasted_iota(jnp.int32, (16, SEQ), 1)
    to_y = lax.rem(2 * y - x + 2 * NY, NY)
    for half in range(2):
        rt[half, 0:HALF] = resid_ref[half * SEQ:(half + 1) * SEQ, :].T
        rt[half, HALF:] = jnp.where(lane < len_ref[half], 1.0, 0.0).astype(BF)
        mine = jnp.logical_and(diag, c == half)

        @pl.when(jnp.logical_not(mine))
        def _():
            rcopy(rt.at[half], rrecv.at[c], s_res.at[half], r_res.at[c], (y, z, to_y, half)).start()

        @pl.when(mine)
        def _():
            rrecv[c] = rt[half]

    @pl.when(diag)
    def _():
        buT[c] = jnp.concatenate([b_ref[...], u_ref[...]], axis=0).T
        gr[c, 0:5] = g_ref[...]
        gr[c, 5:8] = jnp.zeros((3, SEQ), F32)
        for dy in range(1, NY):
            rcopy(buT.at[c], buT.at[c], s_bu.at[dy - 1], r_bu.at[0], dev(0, 0, dy)).start()
            rcopy(gr.at[c], gr.at[c], s_bu.at[dy + 2], r_bu.at[1], dev(0, 0, dy)).start()

    @pl.when(jnp.logical_not(diag))
    def _():
        rcopy(buT.at[c], buT.at[c], s_bu.at[0], r_bu.at[0], dev(0, 0, 1)).wait_recv()
        rcopy(gr.at[c], gr.at[c], s_bu.at[3], r_bu.at[1], dev(0, 0, 1)).wait_recv()

    bu_s = rcopy(buT.at[c], buT.at[c], s_bu.at[6], r_bu.at[2], dev(0, 0, 0, 1))
    gr_s = rcopy(gr.at[c], gr.at[c], s_bu.at[7], r_bu.at[3], dev(0, 0, 0, 1))
    bu_s.start()
    gr_s.start()
    pending.extend([bu_s, gr_s])

    def block(j):
        return lax.rem(x + j, NX)

    def z_item(j):
        xb = block(j)
        zpart[j] = dot(adg[0], ctxg[xb, 0], NT) + dot(adg[1], ctxg[xb, 1], NT)
        dest = lax.rem(x - j + NY, NY)
        dy = lax.rem(dest - y + NY, NY)

        @pl.when(dest != y)
        def _():
            rcopy(zpart.at[j], zb.at[y], s_z.at[j], r_z.at[dy], (x, z, dest, c)).start()

    def mm_item(j, k):
        lo, hi = CHUNKS[k]
        rows = (hi - lo) * COLS
        xb = block(j)
        w0 = wg[0, lo:hi].reshape(rows, HALF)
        w1 = wg[1, lo:hi].reshape(rows, HALF)
        part[j, lo * COLS:hi * COLS] = (dot(w0, ctxg[xb, 0], NT) + dot(w1, ctxg[xb, 1], NT)).astype(BF)
        dest = lax.rem(x - j + NY, NY)
        dy = lax.rem(dest - y + NY, NY)
        piece = pl.ds(lo * COLS, rows)

        @pl.when(dest != y)
        def _():
            rcopy(part.at[j, piece], rsb.at[y, piece], s_rs.at[j, k], r_rs.at[dy, k], (x, z, dest, c)).start()

    def w_wait(s):
        for flow in range(2):
            wr[(s, flow)].wait_recv()
            if s < 8:
                slot = 2 * s - 1 if flow == 0 else 2 * s
                if s < 7 or True:
                    w_start(s + 1, flow, wg.at[c, slot])
                sib.append(w_sib(slot, wg.at[c, slot]))
        if s == 8:
            sib.append(w_sib(15, wg.at[c, 15]))

    def sib_wait(slots):
        for slot in slots:
            rcopy(wg.at[c, slot], wg.at[c, slot], s_ws.at[slot], r_ws.at[slot], dev(0, 0, 0, 1)).wait_recv()

    def ctx_wait(i):
        rcopy(ctxg.at[0, 0], ctxg.at[0, 0], s_ctx.at[4], r_ctx.at[i], dev(0, 0, 0, 1)).wait_recv()

    def ctx_forward(i, dx_src, half_c, to_dx, sem):
        xb = lax.rem(x + dx_src + NX, NX)
        cp = rcopy(ctxg.at[xb, half_c], ctxg.at[xb, half_c], s_ctx.at[sem], r_ctx.at[i], dev(to_dx))
        cp.start()
        pending.append(cp)

    ctx_wait(0)
    ad_cp.wait_recv()
    z_item(0)
    w_wait(1)
    w_wait(2)
    for i in (1, 2, 3, 4):
        ctx_wait(i)
        if i == 1:
            ctx_forward(5, -1, 0, 1, 5)
        if i == 4:
            ctx_forward(6, 1, 1, -1, 6)
    z_item(1)
    z_item(3)
    w_wait(3)
    sib_wait(range(0, 7))
    for j in (0, 1, 3):
        mm_item(j, 0)
    w_wait(4)
    sib_wait((7, 8))
    for j in (0, 1, 3):
        mm_item(j, 1)
    ctx_wait(5)
    ctx_wait(6)
    w_wait(5)
    z_item(2)
    mm_item(2, 0)
    mm_item(2, 1)
    for s in range(5, 9):
        if s > 5:
            w_wait(s)
        sib_wait((9, 10) if s == 5 else ((15,) if s == 8 else (2 * s - 1, 2 * s)))
        for j in (2, 1, 3, 0):
            mm_item(j, s - 3)

    bu_s.wait_recv()
    gr_s.wait_recv()
    for cc in range(2):
        @pl.when(jnp.logical_not(jnp.logical_and(diag, c == cc)))
        def _():
            rcopy(rrecv.at[cc], rrecv.at[cc], s_res.at[cc], r_res.at[cc], dev(0, 0, 0, 1)).wait_recv()
    jown = lax.rem(x - y + NX, NX)
    zz = zpart[jown]
    for dy in range(1, NY):
        ys = lax.rem(y - dy + NY, NY)
        rcopy(zb.at[ys], zb.at[ys], s_z.at[0], r_z.at[dy], dev(0, 0, dy)).wait_recv()
        zz = zz + zb[ys]
    zt = zz[0:RANK]
    ztt = zz[RANK:]
    zero = jnp.zeros((RANK, SEQ), F32)
    rhs = jnp.concatenate([jnp.concatenate([ztt, zt], axis=0), jnp.concatenate([zt, zero], axis=0)], axis=1)
    r1, r2, r3 = split3(rhs)
    for cc in range(2):
        m = buT[cc]
        both = dot(m, r1) + dot(m, r2) + dot(m, r3)
        dh_ref[cc * HALF:(cc + 1) * HALF] = both[:, 0:SEQ]
        h_ref[cc * HALF:(cc + 1) * HALF] = both[:, SEQ:] + rrecv[cc, 0:HALF].astype(F32)
    live = rrecv[0, HALF:].astype(F32)[0:1] * (1.0 / jnp.sqrt(jnp.float32(TOKENS)))

    for k, (lo, hi) in enumerate(CHUNKS):
        for dy in range(1, NY):
            ys = lax.rem(y - dy + NY, NY)
            piece = pl.ds(lo * COLS, (hi - lo) * COLS)
            rcopy(rsb.at[ys, piece], rsb.at[ys, piece], s_rs.at[0, k], r_rs.at[dy, k], dev(0, 0, dy)).wait_recv()
        for slot in range(lo, hi):
            step = (slot + 1) // 2
            zz_ = z if slot == 0 else (z - step if slot % 2 == 1 else z + step)
            zz_ = lax.rem(zz_ + NZ, NZ)
            rows = pl.ds(pl.multiple_of(zz_ * COLS, 16), COLS)
            piece = pl.ds(slot * COLS, COLS)
            acc = part[jown, piece].astype(F32)
            for dy in range(1, NY):
                ys = lax.rem(y - dy + NY, NY)
                acc = acc + rsb[ys, piece].astype(F32)
            h_ref[rows] = h_ref[rows] + acc

    def gsq(i):
        row = gr[i // 5, pl.ds(i % 5, 1)]
        col = jnp.broadcast_to(row, (SEQ, SEQ)).T
        return col * col

    sums = [jnp.zeros((8, SEQ), F32) for _ in range(9)]

    def fold(v):
        return jnp.sum(v.reshape(16, 8, SEQ), axis=0)

    for i in range(10):
        rows = pl.ds(i * SEQ, SEQ)
        h = h_ref[rows]
        d = dh_ref[rows]
        g2 = gsq(i)
        gh_ref[rows] = g2
        hd = h * d
        hh = h * h
        terms = (h, hh, d, hd, g2 * d, g2, g2 * h, g2 * hh, g2 * hd)
        sums = [s + fold(t) for s, t in zip(sums, terms)]
    for n, s in enumerate(sums):
        st_snd[n:n + 1] = jnp.sum(s, axis=0, keepdims=True)
    st_snd[9:] = jnp.zeros((7, SEQ), F32)
    st_cp = []
    for dx in range(1, NX):
        to = (lax.rem(x + dx, NX), z, lax.rem(y + 2 * dx, NY), c)
        cp = rcopy(st_snd, st_rcv.at[dx], s_st.at[dx], r_st.at[dx], to)
        cp.start()
        st_cp.append(cp)
    total = st_snd[...]
    for cp, dx in zip(st_cp, range(1, NX)):
        cp.wait()
        total = total + st_rcv[dx]
    total = total * (1.0 / WIDTH)
    e_h, e_hh, m1, e_hd, e_gd, e_g, e_gh, e_ghh, e_ghd = [total[n:n + 1] for n in range(9)]
    mu = e_h
    rinv = lax.rsqrt(e_hh - mu * mu + 1e-05)
    m2 = rinv * (e_hd - mu * m1)
    g_n = rinv * (e_gh - mu * e_g)
    g_nn = rinv * rinv * (e_ghh - 2.0 * mu * e_gh + mu * mu * e_g)
    g_nd = rinv * (e_ghd - mu * e_gd)
    lr = live * rinv
    m3 = lr * (e_gd - m1 * e_g - m2 * g_n)
    m4 = lr * (g_nd - m1 * g_n - m2 * g_nn)

    q = jnp.zeros((SEQ, 2 * SEQ), F32)
    z1, z2 = split2(zt)
    zs = jnp.concatenate([z1, z2], axis=0)
    for cc in range(2):
        rows = pl.ds(cc * HALF, HALF)
        n = (h_ref[rows] - mu) * rinv
        cot = lr * gh_ref[rows] * (dh_ref[rows] - m1 - n * m2)
        gh = rinv * (cot - m3 - n * m4)
        g1, g2 = split2(gh)
        q = q + dot(buT[cc], jnp.concatenate([g1, g2], axis=1), TN)
        hb = dot(zs, g1, NT) + dot(zs, g2, NT)
        hb = hb[0:RANK] + hb[RANK:]
        for p in range(NX):
            hb_snd[p, cc] = hb[16 * p:16 * (p + 1)]
    mine_b = 2 * x - y
    xq = lax.rem(mine_b + NX, NX)
    qg[xq] = q[0:RANK, 0:SEQ] + q[0:RANK, SEQ:]
    q_cp = []
    for dy in range(1, NY):
        cp = rcopy(qg.at[xq], qg.at[xq], s_q.at[dy], r_q.at[dy], dev(0, 0, dy))
        cp.start()
        q_cp.append(cp)

    for dp in range(NX):
        for dc in range(NC):
            p, cd = lax.rem(x + dp, NX), lax.rem(c + dc, NC)
            me = jnp.logical_and(diag, dp == 0 and dc == 0)

            @pl.when(jnp.logical_not(me))
            def _():
                rcopy(hb_snd.at[p, cd], hb_rcv.at[2 * y + c], s_hb.at[2 * dp + dc], r_hb.at[2 * y + c], (p, z, x, cd)).start()

    @pl.when(diag)
    def _():
        hb_rcv[2 * y + c] = hb_snd[x, c]

    for cp in q_cp:
        cp.wait()
    ha = [jnp.zeros((2 * RANK, HALF), F32) for _ in range(2)]
    for xb in range(NX):
        q1, q2 = split2(qg[xb])
        qs = jnp.concatenate([q1, q2], axis=0)
        ha = [ha[cc] + dot(qs, ctxg[xb, cc]) for cc in range(2)]
    low = lax.broadcasted_iota(jnp.int32, (COLS, SEQ), 1) < RANK
    for cc in range(2):
        t = ha[cc].T
        t = t + pltpu.roll(t, RANK, 1)
        for p in range(NX):
            ha_snd[p, cc] = jnp.where(low, t[160 * p:160 * p + COLS], t[160 * p + COLS:160 * (p + 1)])
    ha_cp = []
    for dx in range(NX):
        for dc in range(NC):
            if (dx, dc) != (0, 0):
                p, cd = lax.rem(x + dx, NX), lax.rem(c + dc, NC)
                i = 2 * dx + dc
                cp = rcopy(ha_snd.at[p, cd], ha_rcv.at[i], s_ha.at[i], r_ha.at[i], (p, z, y, cd))
                cp.start()
                ha_cp.append((i, cp))
    for i in range(8):
        me = jnp.logical_and(diag, 2 * y + c == i)

        @pl.when(jnp.logical_not(me))
        def _():
            rcopy(hb_rcv.at[i], hb_rcv.at[i], s_hb.at[i], r_hb.at[i], dev(0, 0, 0, 1)).wait_recv()
    acc = hb_rcv[0]
    for i in range(1, 8):
        acc = acc + hb_rcv[i]
    hb_sum[...] = acc
    acc = ha_snd[x, c]
    for i, cp in ha_cp:
        cp.wait()
        acc = acc + ha_rcv[i]
    ha_sum[...] = acc
    lowk = lax.broadcasted_iota(jnp.int32, (16, SEQ), 1) < RANK
    for k in range(10):
        a = ha_sum[pl.ds(k, 8, stride=10)]
        a = jnp.concatenate([a, pltpu.roll(a, RANK, 1)], axis=0)
        tile = hb_sum[:, (k // 2) * SEQ:(k // 2 + 1) * SEQ]
        if k % 2 == 0:
            tile = pltpu.roll(tile, RANK, 1)
        v = jnp.where(lowk, a, tile)
        for zi in range(NZ):
            buf2[zi, k:k + 1] = v[zi:zi + 1]
    cps = []
    for dz in range(1, NZ):
        zd = lax.rem(z + dz, NZ)
        cp = rcopy(buf2.at[zd], rcv2.at[dz], s_2.at[dz], r_2.at[dz], dev(0, dz))
        cp.start()
        cps.append(cp)
    acc = buf2[z]
    for dz, cp in zip(range(1, NZ), cps):
        cp.wait()
        acc = acc + rcv2[dz]
    out_a[...] = acc[0:10, 0:RANK]
    for k in range(10):
        out_b[0:1, k * RANK:(k + 1) * RANK] = acc[k:k + 1, RANK:]

    for cp in pending:
        cp.wait_send()
    for half in range(2):
        @pl.when(jnp.logical_not(jnp.logical_and(diag, c == half)))
        def _():
            rcopy(rt.at[half], rrecv.at[c], s_res.at[half], r_res.at[c], (y, z, to_y, half)).wait_send()

    @pl.when(diag)
    def _():
        for dy in range(1, NY):
            rcopy(buT.at[c], buT.at[c], s_bu.at[dy - 1], r_bu.at[0], dev(0, 0, dy)).wait_send()
            rcopy(gr.at[c], gr.at[c], s_bu.at[dy + 2], r_bu.at[1], dev(0, 0, dy)).wait_send()

    for j in range(NX):
        dest = lax.rem(x - j + NY, NY)

        @pl.when(dest != y)
        def _():
            rcopy(zpart.at[j], zb.at[y], s_z.at[j], r_z.at[0], (x, z, dest, c)).wait_send()
            for k, (lo, hi) in enumerate(CHUNKS):
                piece = pl.ds(lo * COLS, (hi - lo) * COLS)
                rcopy(part.at[j, piece], rsb.at[y, piece], s_rs.at[j, k], r_rs.at[0, k], (x, z, dest, c)).wait_send()
    for dp in range(NX):
        for dc in range(NC):
            p, cd = lax.rem(x + dp, NX), lax.rem(c + dc, NC)
            me = jnp.logical_and(diag, dp == 0 and dc == 0)

            @pl.when(jnp.logical_not(me))
            def _():
                rcopy(hb_snd.at[p, cd], hb_rcv.at[2 * y + c], s_hb.at[2 * dp + dc], r_hb.at[2 * y + c], (p, z, x, cd)).wait_send()


def body(ctx, resid, w, a, b, d, u, gain, lengths):
    vmem = pl.BlockSpec(memory_space=pltpu.VMEM)
    dma = lambda *n: pltpu.SemaphoreType.DMA(n)
    return pl.pallas_call(
        kernel,
        out_shape=(jax.ShapeDtypeStruct((10, RANK), F32), jax.ShapeDtypeStruct((1, HALF), F32)),
        in_specs=[vmem] * 8 + [pl.BlockSpec(memory_space=pltpu.SMEM)],
        out_specs=(vmem, vmem),
        scratch_shapes=[
            pltpu.VMEM((NX, NC, SEQ, HALF), BF),
            pltpu.VMEM((NC, NZ, COLS, HALF), BF),
            pltpu.VMEM((NC, 2 * RANK, HALF), BF),
            pltpu.VMEM((2, HALF + 16, SEQ), BF),
            pltpu.VMEM((2, HALF + 16, SEQ), BF),
            pltpu.VMEM((NC, HALF, SEQ), BF),
            pltpu.VMEM((NC, 8, SEQ), F32),
            pltpu.VMEM((NX, FEATS, SEQ), BF),
            pltpu.VMEM((NY, FEATS, SEQ), BF),
            pltpu.VMEM((NX, SEQ, SEQ), F32),
            pltpu.VMEM((NY, SEQ, SEQ), F32),
            pltpu.VMEM((FEATS, SEQ), F32),
            pltpu.VMEM((FEATS, SEQ), F32),
            pltpu.VMEM((FEATS, SEQ), F32),
            pltpu.VMEM((16, SEQ), F32),
            pltpu.VMEM((NX, 16, SEQ), F32),
            pltpu.VMEM((NX, RANK, SEQ), F32),
            pltpu.VMEM((NX, NC, COLS, SEQ), F32),
            pltpu.VMEM((8, COLS, SEQ), F32),
            pltpu.VMEM((NX, NC, 16, HALF), F32),
            pltpu.VMEM((8, 16, HALF), F32),
            pltpu.VMEM((COLS, SEQ), F32),
            pltpu.VMEM((16, HALF), F32),
            pltpu.VMEM((NZ, 16, SEQ), F32),
            pltpu.VMEM((NZ, 16, SEQ), F32),
            dma(7), dma(7), dma(16), dma(16), dma(16), dma(16), dma(1), dma(1), dma(2), dma(2), dma(8), dma(4),
            dma(NX, NCH), dma(NY, NCH), dma(NX), dma(NY), dma(NX), dma(NX), dma(NY), dma(NY), dma(8), dma(8),
            dma(8), dma(8), dma(NZ), dma(NZ),
        ],
        compiler_params=pltpu.CompilerParams(collective_id=0, has_side_effects=True, vmem_limit_bytes=40 << 20),
        cost_estimate=pl.CostEstimate(flops=2 * 1280 * 1280 * 512, bytes_accessed=2 << 20, transcendentals=0),
        name="hvp",
    )(ctx, resid, w.T, a.T, d.T, b, u, gain.reshape(5, SEQ), lengths)


def solution(mesh):
    grid = Mesh(mesh.devices.reshape(NX, NZ, NY, NC), AXES)
    dp, tensor = ("x", "z"), ("y", "c")
    in_specs = (
        P(dp, tensor),
        P(dp, tensor),
        P(tensor, dp),
        P(tensor, None),
        P(None, tensor),
        P(tensor, None),
        P(None, tensor),
        P(tensor),
        P(dp),
    )
    out_specs = (P(("y", "c", "x", "z"), None), P(dp, tensor))
    return jax.shard_map(body, mesh=grid, in_specs=in_specs, out_specs=out_specs, check_vma=False)
```

time: 606 us -> 118 us (0.19); the launches traced: 596 us -> 117 us
  waiting for transfers between devices: 512 us -> 0 us
  Pallas kernels: 0 us -> 109 us
  blocking collectives: 40.6 us -> 0 us
  matrix products: 17 us -> 0 us
  between operations: 16.4 us -> 0.67 us
    unnamed x7 -> x0, waiting for transfers between devices: 294 us -> none
    all_gather x1 -> x0, waiting for transfers between devices: 149 us -> none  [body(): lax.all_gather(output_projection_weight, 'dp', axis=1, tiled=True)]
    pallas_call x0 -> x1, Pallas kernels: none -> 109 us  [body(): pl.pallas_call(kernel, out_shape=(jax.ShapeDtypeStruct((10, RANK), F32),...]
    psum x2 -> x0, waiting for transfers between devices: 69.4 us -> none  [the longest x1 69.4 us: body(): lax.psum(jnp.dot(grad_h, raised_output.T, precision=high), 'tensor')]
    psum x3 -> x0, blocking collectives: 40.6 us -> none  [the longest x1 14.3 us: body(): lax.psum((jnp.sum(hidden, axis=1, keepdims=True), jnp.sum(hidden * hidden...]
    dot_general x9 -> x0, matrix products: 17 us -> none  [the longest x1 5.09 us: body(): jnp.dot(ctx, lax.all_gather(output_projection_weight, 'dp', axis=1, tiled...]
  transfers between devices with their start and end apart: 5 -> 0, of which waited for: 4 -> 0; matrix products, arithmetic and copies ran while one was open for 3% -> 0% of each run, Pallas kernels for 0% -> 0%
where the time goes in v1:
time: 118 us; the launch traced here: 117 us
  Pallas kernels  109 us (92%)
  local copies, waits for them, and re-layouts  8.24 us (7%)
    pallas_call x1, Pallas kernels, body(): pl.pallas_call(kernel, out_shape=(jax.ShapeDtypeStruct((10, RANK), F32),...  109 us
    unnamed x20, local copies, waits for them, and re-layouts  8.24 us

profile of v1, /device:TPU:1, one launch (start us, length us, event | category | flops | bytes accessed | tf_op | source)
XLA Modules:
  0.0 117.4 jit_solution(3188491785781542233)
XLA Ops:
  0.6 0.0 copy-start.7
  0.6 0.0 copy-start.8
  0.7 0.7 copy-done.7
  1.3 0.0 copy-done.8
  1.3 0.0 copy-start
  1.3 1.0 copy-done
  2.3 0.0 copy-start.1
  2.3 1.0 copy-done.1
  3.3 0.0 copy-start.2
  3.3 0.9 copy-done.2
  4.2 0.0 copy-start.3
  4.2 0.9 copy-done.3
  5.1 0.0 copy-start.4
  5.1 0.9 copy-done.4
  5.9 0.0 copy-start.5
  5.9 0.9 copy-done.5
  6.8 0.0 copy-start.6
  6.8 0.9 copy-done.6
  7.7 108.5 %hvp.1 = (f32[10,64]{1,0:T(8,128)S(1)}, f32[1,640]{1,0:T(1,128)S(1)}) custom-call(bf16[256,640]{1,0:T(8,128)(2,1)S(1)} %copy-done, bf16[256,640]{1,0:T(8,128)(2,1)S(1)} %copy-done.1, bf16[80,640]{1,0:T(8,128)(2,1)S(1)} %bitcast.4, bf16[64,640]{1,0:T(8,128)(2,1)S(1)} %bitcast.5, bf16[64,640]{1,0:T(8,128)(2,1)S(1)} %bitcast.6, bf16[64,640]{1,0:T(8,128)(2,1)S(1)} %copy-done.5, ...), custom_call_target="tpu_custom_call" | custom-call | flops 1677721600 | bytes 2097152 | tf_op jit(solution)/shard_map/hvp/pallas_call | solution.py:462
  116.2 0.6 copy.13
  116.8 0.6 copy.14
Async XLA Ops:
  0.6 0.7 copy-start.7
  0.6 0.7 copy-start.8
  1.3 1.0 copy-start
  2.3 1.0 copy-start.1
  3.3 0.9 copy-start.2
  4.2 0.9 copy-start.3
  5.1 0.9 copy-start.4
  5.9 0.9 copy-start.5
  6.8 0.9 copy-start.6

commit v2 on v0

v2 whole, which is shorter than its diff:
```python
import functools

import jax
import jax.numpy as jnp
from jax import lax
from jax.experimental import pallas as pl
from jax.experimental.pallas import tpu as pltpu
from jax.sharding import Mesh, PartitionSpec as P

AXES = ("x", "z", "y", "c")
NX, NZ, NY, NC = 4, 16, 4, 2
SEQ = 128
RANK = 64
FEATS = 1280
HALF = 640
COLS = 80
TOKENS = 16384
WIDTH = 5120
BF = jnp.bfloat16
F32 = jnp.float32
CHUNKS = ((0, 1),) + tuple((2 * s - 1, 2 * s + 1) for s in range(1, 8)) + ((15, 16),)
PARTS = ((0, 48), (48, 32))
NCH = len(CHUNKS)
NT = (((1,), (1,)), ((), ()))
TN = (((0,), (0,)), ((), ()))


def split2(v):
    hi = v.astype(BF)
    lo = (v - hi.astype(F32)).astype(BF)
    return hi, lo


def split3(v):
    hi = v.astype(BF)
    rest = v - hi.astype(F32)
    mid = rest.astype(BF)
    lo = (rest - mid.astype(F32)).astype(BF)
    return hi, mid, lo


def dot(a, b, dims=(((1,), (0,)), ((), ()))):
    return lax.dot_general(a, b, dims, preferred_element_type=F32)


def kernel(
    ctx_ref, resid_ref, wt_ref, at_ref, dt_ref, b_ref, u_ref, g_ref, len_ref,
    out_a, out_b,
    ctx_v, resid_v, bu_v, g_v, len_v,
    ctxs, ctxg, wg, adg, rt, relay, rrecv, buT, gr, part, rsb, zp, zr, zsum, zall, h_ref, dh_ref, gh_ref,
    st_snd, st_rcv, qg, ha_snd, ha_rcv, hb_snd, hb_sib, hb_red, hb_rcv, ha_sum, hb2, hbz, ha2, haz,
    s_in, s_ctx, r_ctx, s_w, r_w, s_ws, r_ws, s_ad, r_ad, s_res, r_res, s_rel, r_rel, s_bu, r_bu, s_rs, r_rs,
    s_zr, r_zr, s_zd, r_zd, s_st, r_st, s_q, r_q, s_ha, r_ha, s_hs, r_hs, s_hb, r_hb, s_bz, r_bz, s_az, r_az,
):
    x, z, y, c = [lax.axis_index(a) for a in AXES]
    other = lax.rem(c + 1, NC)
    diag = x == y

    def mod4(v):
        return lax.rem(v + 8, 4)

    def dev(dx=0, dz=0, dy=0, dc=0):
        return (mod4(x + dx), lax.rem(z + dz + NZ, NZ), mod4(y + dy), lax.rem(c + dc, NC))

    def rcopy(src, dst, ss, rs, to):
        return pltpu.make_async_remote_copy(
            src_ref=src, dst_ref=dst, send_sem=ss, recv_sem=rs, device_id=to, device_id_type=pl.DeviceIdType.MESH
        )

    def arrived(dst, rs):
        rcopy(dst, dst, s_ad.at[0], rs, dev(0, 0, 0, 1)).wait_recv()

    pending = []

    def send(src, dst, ss, rs, to):
        cp = rcopy(src, dst, ss, rs, to)
        cp.start()
        pending.append((None, cp))

    def send_unless(cond, src, dst, ss, rs, to):
        cp = rcopy(src, dst, ss, rs, to)
        keep = jnp.logical_not(cond)

        @pl.when(keep)
        def _():
            cp.start()

        pending.append((keep, cp))

    loads = [
        pltpu.make_async_copy(src, dst, s_in.at[i])
        for i, (src, dst) in enumerate((
            (wt_ref, wg.at[c, 0]),
            (ctx_ref, ctx_v),
            (at_ref, adg.at[c, pl.ds(0, RANK)]),
            (dt_ref, adg.at[c, pl.ds(RANK, RANK)]),
            (resid_ref, resid_v),
            (b_ref, bu_v.at[pl.ds(0, RANK)]),
            (u_ref, bu_v.at[pl.ds(RANK, RANK)]),
            (g_ref, g_v),
            (len_ref, len_v),
        ))
    ]
    for cp in loads:
        cp.start()

    barrier = pltpu.get_barrier_semaphore()
    count = 0
    for dx in range(NX):
        for dy in range(NY):
            for dc in range(NC):
                if (dx, dy, dc) != (0, 0, 0):
                    pl.semaphore_signal(barrier, inc=1, device_id=dev(dx, 0, dy, dc), device_id_type=pl.DeviceIdType.MESH)
                    count += 1
    for dz in range(1, NZ):
        pl.semaphore_signal(barrier, inc=1, device_id=dev(0, dz), device_id_type=pl.DeviceIdType.MESH)
        count += 1
    loads[1].wait()
    for half in range(2):
        ctxs[half] = ctx_v[half * SEQ:(half + 1) * SEQ, :].T
    loads[0].wait()
    pl.semaphore_wait(barrier, count)

    def w_copy(s, flow, sub):
        if s == 8:
            src, dst = 13 + flow, 15
        else:
            src, dst = (0 if s == 1 else 2 * s - 3 + flow), 2 * s - 1 + flow
        rows = pl.ds(*PARTS[sub])
        k = 4 * (s - 1) + 2 * flow + sub
        return rcopy(wg.at[c, src, rows], wg.at[c, dst, rows], s_w.at[k], r_w.at[k], dev(0, 1 - 2 * flow))

    def w_start(s, flow, sub):
        cp = w_copy(s, flow, sub)
        cp.start()
        pending.append((None, cp))

    def w_sib(slot):
        send(wg.at[c, slot], wg.at[c, slot], s_ws.at[slot], r_ws.at[slot], dev(0, 0, 0, 1))

    for sub in range(2):
        for flow in range(2):
            w_start(1, flow, sub)
    for half in range(2):
        for k, dx in ((1, 1), (3, -1)):
            send(ctxs.at[half], ctxg.at[x, c], s_ctx.at[k - 1 + half], r_ctx.at[k + c], (mod4(x + dx), z, y, half))
    send(ctxs.at[other], ctxg.at[x, c], s_ctx.at[4], r_ctx.at[0], dev(0, 0, 0, 1))
    w_sib(0)
    loads[2].wait()
    loads[3].wait()
    send(adg.at[c], adg.at[c], s_ad.at[0], r_ad.at[0], dev(0, 0, 0, 1))
    ctxg[x, c] = ctxs[c]

    loads[4].wait()
    loads[8].wait()
    lane = lax.broadcasted_iota(jnp.int32, (16, SEQ), 1)
    kq = y // 2
    for half in range(2):
        rt[half, 0:HALF] = resid_v[half * SEQ:(half + 1) * SEQ, :].T
        rt[half, HALF:] = jnp.where(lane < len_v[half], 1.0, 0.0).astype(BF)
        mine = jnp.logical_and(diag, c == half)
        send_unless(mine, rt.at[half], relay.at[kq, c], s_res.at[half], r_res.at[kq, c], (x, z, mod4(2 * y - x), half))

        @pl.when(mine)
        def _():
            relay[kq, c] = rt[half]

    for i in (5, 6, 7):
        loads[i].wait()
    off = jnp.logical_not(diag)

    @pl.when(diag)
    def _():
        buT[c] = bu_v[...].T
        gr[c] = jnp.concatenate([g_v[...], jnp.zeros((3, SEQ), F32)], axis=0)

    for dy in range(1, NY):
        send_unless(off, buT.at[c], buT.at[c], s_bu.at[dy - 1], r_bu.at[0], dev(0, 0, dy))
        send_unless(off, gr.at[c], gr.at[c], s_bu.at[dy + 2], r_bu.at[1], dev(0, 0, dy))

    def block(j):
        return mod4(x + j)

    def mm(js, k):
        lo, hi = CHUNKS[k]
        rows = (hi - lo) * COLS
        rhs = [jnp.concatenate([ctxg[block(j), cc] for j in js], axis=1) for cc in range(2)]
        lhs = [wg[cc, lo:hi].reshape(rows, HALF) for cc in range(2)]
        out = (dot(lhs[0], rhs[0]) + dot(lhs[1], rhs[1])).astype(BF)
        piece = pl.ds(lo * COLS, rows)
        for i, j in enumerate(js):
            part[j, piece] = out[:, i * SEQ:(i + 1) * SEQ]
            dest = mod4(x - j)
            send_unless(
                dest == y, part.at[j, piece], rsb.at[y, piece], s_rs.at[j, k], r_rs.at[mod4(dest - y), k], (x, z, dest, c)
            )

    def w_take(s, sub):
        for flow in range(2):
            if s < 8 or flow == sub:
                w_copy(s, flow, sub).wait_recv()
                if s < 7 or (s == 7 and flow == sub):
                    w_start(s + 1, flow, sub)
        if sub == 1:
            for slot in range(2 * s - 1, min(2 * s + 1, NZ)):
                w_sib(slot)

    def sib_wait(k):
        for slot in range(*CHUNKS[k]):
            arrived(wg.at[c, slot], r_ws.at[slot])

    def ctx_forward(i, dx_src, half_c, to_dx, sem):
        blk = ctxg.at[mod4(x + dx_src), half_c]
        send(blk, blk, s_ctx.at[sem], r_ctx.at[i], dev(to_dx))

    def ctx_wait(i):
        arrived(ctxg.at[0, 0], r_ctx.at[i])

    w_take(1, 0)
    ctx_wait(0)
    arrived(adg.at[c], r_ad.at[0])
    w_take(1, 1)
    zp[...] = dot(adg[0], ctxg[x, 0]) + dot(adg[1], ctxg[x, 1])
    zp_rows = lambda yy: zp.at[pl.ds(pl.multiple_of(yy * 32, 32), 32)]
    for dy in range(1, NY):
        yd = mod4(y + dy)
        send(zp_rows(yd), zr.at[dy], s_zr.at[dy], r_zr.at[dy], dev(0, 0, dy))
    sib_wait(0)
    mm((0,), 0)
    w_take(2, 0)
    w_take(2, 1)
    sib_wait(1)
    mm((0,), 1)
    w_take(3, 0)
    w_take(3, 1)
    sib_wait(2)
    mm((0,), 2)
    ctx_wait(1)
    ctx_forward(5, -1, 0, 1, 5)
    ctx_wait(4)
    ctx_forward(6, 1, 1, -1, 6)
    ctx_wait(2)
    ctx_wait(3)
    mm((1, 3), 0)
    mm((1, 3), 1)
    mm((1, 3), 2)
    w_take(4, 0)
    w_take(4, 1)
    sib_wait(3)
    mm((0, 1, 3), 3)
    acc = zp[pl.ds(pl.multiple_of(y * 32, 32), 32)]
    for dy in range(1, NY):
        arrived(zr.at[dy], r_zr.at[dy])
        acc = acc + zr[dy]
    zsum[...] = acc
    for dq in range(NX):
        me = jnp.logical_and(diag, dq == 0)
        send_unless(me, zsum, zall.at[y], s_zd.at[dq], r_zd.at[y], (mod4(x + dq), z, mod4(x + 2 * dq), c))

    @pl.when(diag)
    def _():
        zall[y] = acc

    w_take(5, 0)
    w_take(5, 1)
    sib_wait(4)
    mm((0, 1, 3), 4)
    is_relay = (x + y) % 2 == 0
    q0 = lax.rem((x + y) // 2, 2)
    for k in range(2):
        q = q0 + 2 * k
        for cc in range(2):
            own = jnp.logical_and(diag, jnp.logical_and(kq == k, c == cc))
            here = jnp.logical_and(is_relay, jnp.logical_not(own))

            @pl.when(here)
            def _():
                arrived(relay.at[k, cc], r_res.at[k, cc])

            stay = q == x
            send_unless(
                jnp.logical_not(jnp.logical_and(is_relay, q != x)),
                relay.at[k, cc], rrecv.at[cc], s_rel.at[k, cc], r_rel.at[cc], (q, z, y, c),
            )

            @pl.when(jnp.logical_and(is_relay, stay))
            def _():
                rrecv[cc] = relay[k, cc]

    ctx_wait(5)
    ctx_wait(6)
    mm((2,), 0)
    mm((2,), 1)
    mm((2,), 2)
    w_take(6, 0)
    w_take(6, 1)
    mm((2,), 3)
    mm((2,), 4)
    sib_wait(5)
    mm((0, 1, 2, 3), 5)

    @pl.when(off)
    def _():
        arrived(buT.at[c], r_bu.at[0])
        arrived(gr.at[c], r_bu.at[1])

    send(buT.at[c], buT.at[c], s_bu.at[6], r_bu.at[2], dev(0, 0, 0, 1))
    send(gr.at[c], gr.at[c], s_bu.at[7], r_bu.at[3], dev(0, 0, 0, 1))
    w_take(7, 0)
    w_take(7, 1)
    sib_wait(6)
    mm((0, 1, 2, 3), 6)
    w_take(8, 0)
    w_take(8, 1)
    sib_wait(7)
    mm((0, 1, 2, 3), 7)
    sib_wait(8)
    mm((0, 1, 2, 3), 8)

    for ys in range(NY):
        @pl.when(jnp.logical_not(jnp.logical_and(diag, y == ys)))
        def _():
            arrived(zall.at[ys], r_zd.at[ys])

    arrived(buT.at[c], r_bu.at[2])
    arrived(gr.at[c], r_bu.at[3])
    zt = jnp.concatenate([zall[0], zall[1]], axis=0)
    ztt = jnp.concatenate([zall[2], zall[3]], axis=0)
    zero = jnp.zeros((RANK, SEQ), F32)
    rhs = jnp.concatenate([jnp.concatenate([ztt, zt], axis=0), jnp.concatenate([zt, zero], axis=0)], axis=1)
    r1, r2, r3 = split3(rhs)
    for cc in range(2):
        m = buT[cc]
        both = dot(m, r1) + dot(m, r2) + dot(m, r3)
        dh_ref[cc * HALF:(cc + 1) * HALF] = both[:, 0:SEQ]
        h_ref[cc * HALF:(cc + 1) * HALF] = both[:, SEQ:]

    for cc in range(2):
        @pl.when(off)
        def _():
            arrived(rrecv.at[cc], r_rel.at[cc])
        h_ref[cc * HALF:(cc + 1) * HALF] = h_ref[cc * HALF:(cc + 1) * HALF] + rrecv[cc, 0:HALF].astype(F32)
    live = rrecv[0, HALF:].astype(F32)[0:1] * (1.0 / jnp.sqrt(jnp.float32(TOKENS)))

    jown = mod4(x - y)
    for k, (lo, hi) in enumerate(CHUNKS):
        for dy in range(1, NY):
            piece = pl.ds(lo * COLS, (hi - lo) * COLS)
            arrived(rsb.at[mod4(y - dy), piece], r_rs.at[dy, k])
        for slot in range(lo, hi):
            step = (slot + 1) // 2
            zz = z if slot == 0 else (z - step if slot % 2 == 1 else z + step)
            zz = lax.rem(zz + NZ, NZ)
            rows = pl.ds(pl.multiple_of(zz * COLS, 16), COLS)
            piece = pl.ds(slot * COLS, COLS)
            acc = part[jown, piece].astype(F32)
            for dy in range(1, NY):
                acc = acc + rsb[mod4(y - dy), piece].astype(F32)
            h_ref[rows] = h_ref[rows] + acc

    def gsq(i):
        row = gr[i // 5, pl.ds(i % 5, 1)]
        col = jnp.broadcast_to(row, (SEQ, SEQ)).T
        return col * col

    sums = [jnp.zeros((8, SEQ), F32) for _ in range(9)]

    def fold(v):
        return jnp.sum(v.reshape(16, 8, SEQ), axis=0)

    for i in range(10):
        rows = pl.ds(i * SEQ, SEQ)
        h = h_ref[rows]
        d = dh_ref[rows]
        g2 = gsq(i)
        gh_ref[rows] = g2
        hd = h * d
        hh = h * h
        terms = (h, hh, d, hd, g2 * d, g2, g2 * h, g2 * hh, g2 * hd)
        sums = [s + fold(t) for s, t in zip(sums, terms)]
    for n, s in enumerate(sums):
        st_snd[n:n + 1] = jnp.sum(s, axis=0, keepdims=True)
    st_snd[9:] = jnp.zeros((7, SEQ), F32)
    for dx in range(1, NX):
        send(st_snd, st_rcv.at[dx], s_st.at[dx], r_st.at[dx], (mod4(x + dx), z, mod4(y + 2 * dx), c))
    total = st_snd[...]
    for dx in range(1, NX):
        arrived(st_rcv.at[dx], r_st.at[dx])
        total = total + st_rcv[dx]
    total = total * (1.0 / WIDTH)
    mu, e_hh, m1, e_hd, e_gd, e_g, e_gh, e_ghh, e_ghd = [total[n:n + 1] for n in range(9)]
    rinv = lax.rsqrt(e_hh - mu * mu + 1e-05)
    m2 = rinv * (e_hd - mu * m1)
    g_n = rinv * (e_gh - mu * e_g)
    g_nn = rinv * rinv * (e_ghh - 2.0 * mu * e_gh + mu * mu * e_g)
    g_nd = rinv * (e_ghd - mu * e_gd)
    lr = live * rinv
    m3 = lr * (e_gd - m1 * e_g - m2 * g_n)
    m4 = lr * (g_nd - m1 * g_n - m2 * g_nn)

    q = jnp.zeros((SEQ, 2 * SEQ), F32)
    parts = []
    for cc in range(2):
        rows = pl.ds(cc * HALF, HALF)
        n = (h_ref[rows] - mu) * rinv
        cot = lr * gh_ref[rows] * (dh_ref[rows] - m1 - n * m2)
        g1, g2 = split2(rinv * (cot - m3 - n * m4))
        parts.append((g1, g2))
        q = q + dot(buT[cc], jnp.concatenate([g1, g2], axis=1), TN)
    xq = mod4(2 * x - y)
    q1, q2 = split2(q[0:RANK, 0:SEQ] + q[0:RANK, SEQ:])
    qg[xq] = jnp.concatenate([q1, q2], axis=0).T
    for dy in range(1, NY):
        send(qg.at[xq], qg.at[xq], s_q.at[dy], r_q.at[dy], dev(0, 0, dy))

    z1, z2 = split2(zt)
    zs = jnp.concatenate([z1, z2], axis=0)
    for cc in range(2):
        g1, g2 = parts[cc]
        hb = dot(zs, g1, NT) + dot(zs, g2, NT)
        hb = hb[0:RANK] + hb[RANK:]
        for p in range(NX):
            hb_snd[cc, p] = hb[16 * p:16 * (p + 1)]
    send(hb_snd.at[other], hb_sib, s_hs.at[0], r_hs.at[0], dev(0, 0, 0, 1))
    arrived(hb_sib, r_hs.at[0])
    hb_red[...] = hb_snd[c] + hb_sib[...]
    for dp in range(NX):
        p = mod4(x + dp)
        me = jnp.logical_and(diag, dp == 0)
        send_unless(me, hb_red.at[p], hb_rcv.at[y], s_hb.at[dp], r_hb.at[y], (p, z, x, c))

    @pl.when(diag)
    def _():
        hb_rcv[y] = hb_red[x]

    for dy in range(1, NY):
        arrived(qg.at[xq], r_q.at[dy])
    qs = jnp.concatenate([qg[xb] for xb in range(NX)], axis=0)
    low = lax.broadcasted_iota(jnp.int32, (COLS, SEQ), 1) < RANK
    for cc in range(2):
        t = dot(jnp.concatenate([ctxg[xb, cc] for xb in range(NX)], axis=1), qs)
        t = t + pltpu.roll(t, RANK, 1)
        for p in range(NX):
            ha_snd[p, cc] = jnp.where(low, t[160 * p:160 * p + COLS], t[160 * p + COLS:160 * (p + 1)])
    for dx in range(NX):
        for dc in range(NC):
            if (dx, dc) != (0, 0):
                p, cd = mod4(x + dx), lax.rem(c + dc, NC)
                i = 2 * dx + dc
                send(ha_snd.at[p, cd], ha_rcv.at[i], s_ha.at[i], r_ha.at[i], (p, z, y, cd))
    for ys in range(NY):
        @pl.when(jnp.logical_not(jnp.logical_and(diag, y == ys)))
        def _():
            arrived(hb_rcv.at[ys], r_hb.at[ys])
    acc = hb_rcv[0] + hb_rcv[1] + hb_rcv[2] + hb_rcv[3]
    for k in range(5):
        tile = acc[:, k * SEQ:(k + 1) * SEQ]
        for zi in range(NZ):
            hb2[zi, k:k + 1] = tile[zi:zi + 1]
    for dz in range(1, NZ):
        send(hb2.at[lax.rem(z + dz, NZ)], hbz.at[dz], s_bz.at[dz], r_bz.at[dz], dev(0, dz))
    acc = ha_snd[x, c]
    for i in range(1, 8):
        arrived(ha_rcv.at[i], r_ha.at[i])
        acc = acc + ha_rcv[i]
    ha_sum[...] = acc
    low = lax.broadcasted_iota(jnp.int32, (8, SEQ), 1) < RANK
    for k in range(5):
        a = ha_sum[pl.ds(k, 8, stride=10)]
        b = ha_sum[pl.ds(k + 5, 8, stride=10)]
        v = jnp.where(low, a, pltpu.roll(b, RANK, 1))
        w = jnp.where(low, pltpu.roll(a, RANK, 1), b)
        for zi in range(8):
            ha2[zi, k:k + 1] = v[zi:zi + 1]
            ha2[zi + 8, k:k + 1] = w[zi:zi + 1]
    for dz in range(1, NZ):
        send(ha2.at[lax.rem(z + dz, NZ)], haz.at[dz], s_az.at[dz], r_az.at[dz], dev(0, dz))
    acc = hb2[z]
    for dz in range(1, NZ):
        arrived(hbz.at[dz], r_bz.at[dz])
        acc = acc + hbz[dz]
    for k in range(5):
        out_b[0:1, k * SEQ:(k + 1) * SEQ] = acc[k:k + 1]
    acc = ha2[z]
    for dz in range(1, NZ):
        arrived(haz.at[dz], r_az.at[dz])
        acc = acc + haz[dz]
    out_a[0:5] = acc[0:5, 0:RANK]
    out_a[5:10] = acc[0:5, RANK:]

    for keep, cp in pending:
        if keep is None:
            cp.wait_send()
        else:
            @pl.when(keep)
            def _():
                cp.wait_send()


def body(ctx, resid, w, a, b, d, u, gain, lengths):
    vmem = pl.BlockSpec(memory_space=pltpu.VMEM)
    dma = lambda *n: pltpu.SemaphoreType.DMA(n)
    return pl.pallas_call(
        kernel,
        out_shape=(jax.ShapeDtypeStruct((10, RANK), F32), jax.ShapeDtypeStruct((1, HALF), F32)),
        in_specs=[pl.BlockSpec(memory_space=pl.ANY)] * 9,
        out_specs=(vmem, vmem),
        scratch_shapes=[
            pltpu.VMEM((2 * SEQ, HALF), BF),
            pltpu.VMEM((2 * SEQ, HALF), BF),
            pltpu.VMEM((2 * RANK, HALF), BF),
            pltpu.VMEM((5, SEQ), F32),
            pltpu.SMEM((2,), jnp.int32),
            pltpu.VMEM((2, HALF, SEQ), BF),
            pltpu.VMEM((NX, NC, HALF, SEQ), BF),
            pltpu.VMEM((NC, NZ, COLS, HALF), BF),
            pltpu.VMEM((NC, 2 * RANK, HALF), BF),
            pltpu.VMEM((2, HALF + 16, SEQ), BF),
            pltpu.VMEM((2, 2, HALF + 16, SEQ), BF),
            pltpu.VMEM((2, HALF + 16, SEQ), BF),
            pltpu.VMEM((NC, HALF, SEQ), BF),
            pltpu.VMEM((NC, 8, SEQ), F32),
            pltpu.VMEM((NX, FEATS, SEQ), BF),
            pltpu.VMEM((NY, FEATS, SEQ), BF),
            pltpu.VMEM((SEQ, SEQ), F32),
            pltpu.VMEM((NY, 32, SEQ), F32),
            pltpu.VMEM((32, SEQ), F32),
            pltpu.VMEM((NY, 32, SEQ), F32),
            pltpu.VMEM((FEATS, SEQ), F32),
            pltpu.VMEM((FEATS, SEQ), F32),
            pltpu.VMEM((FEATS, SEQ), F32),
            pltpu.VMEM((16, SEQ), F32),
            pltpu.VMEM((NX, 16, SEQ), F32),
            pltpu.VMEM((NX, SEQ, SEQ), BF),
            pltpu.VMEM((NX, NC, COLS, SEQ), F32),
            pltpu.VMEM((8, COLS, SEQ), F32),
            pltpu.VMEM((NC, NX, 16, HALF), F32),
            pltpu.VMEM((NX, 16, HALF), F32),
            pltpu.VMEM((NX, 16, HALF), F32),
            pltpu.VMEM((NY, 16, HALF), F32),
            pltpu.VMEM((COLS, SEQ), F32),
            pltpu.VMEM((NZ, 8, SEQ), F32),
            pltpu.VMEM((NZ, 8, SEQ), F32),
            pltpu.VMEM((NZ, 8, SEQ), F32),
            pltpu.VMEM((NZ, 8, SEQ), F32),
            dma(9),
            dma(7), dma(7), dma(32), dma(32), dma(16), dma(16), dma(1), dma(1), dma(2), dma(2, 2), dma(2, 2), dma(2),
            dma(8), dma(4), dma(NX, NCH), dma(NY, NCH),
            dma(NY), dma(NY), dma(NX), dma(NY), dma(NX), dma(NX), dma(NY), dma(NY), dma(8), dma(8), dma(1), dma(1),
            dma(NX), dma(NY), dma(NZ), dma(NZ), dma(NZ), dma(NZ),
        ],
        compiler_params=pltpu.CompilerParams(collective_id=0, has_side_effects=True, vmem_limit_bytes=40 << 20),
        cost_estimate=pl.CostEstimate(flops=2 * 1280 * 1280 * 512, bytes_accessed=2 << 20, transcendentals=0),
        name="hvp",
    )(ctx, resid, w.T, a.T, d.T, b, u, gain.reshape(5, SEQ), lengths)


def solution(mesh):
    grid = Mesh(mesh.devices.reshape(NX, NZ, NY, NC), AXES)
    dp, tensor = ("x", "z"), ("y", "c")
    in_specs = (
        P(dp, tensor),
        P(dp, tensor),
        P(tensor, dp),
        P(tensor, None),
        P(None, tensor),
        P(tensor, None),
        P(None, tensor),
        P(tensor),
        P(dp),
    )
    out_specs = (P(("y", "c", "x", "z"), None), P(dp, tensor))
    return jax.shard_map(body, mesh=grid, in_specs=in_specs, out_specs=out_specs, check_vma=False)
```

time: 606 us -> 89.1 us (0.15); the launches traced: 596 us -> 88.7 us
  waiting for transfers between devices: 512 us -> 0 us
  Pallas kernels: 0 us -> 79.8 us
  blocking collectives: 40.6 us -> 0 us
  matrix products: 17 us -> 0 us
  between operations: 16.4 us -> 0.67 us
    unnamed x7 -> x0, waiting for transfers between devices: 294 us -> none
    all_gather x1 -> x0, waiting for transfers between devices: 149 us -> none  [body(): lax.all_gather(output_projection_weight, 'dp', axis=1, tiled=True)]
    pallas_call x0 -> x1, Pallas kernels: none -> 79.8 us  [body(): pl.pallas_call(kernel, out_shape=(jax.ShapeDtypeStruct((10, RANK), F32),...]
    psum x2 -> x0, waiting for transfers between devices: 69.4 us -> none  [the longest x1 69.4 us: body(): lax.psum(jnp.dot(grad_h, raised_output.T, precision=high), 'tensor')]
    psum x3 -> x0, blocking collectives: 40.6 us -> none  [the longest x1 14.3 us: body(): lax.psum((jnp.sum(hidden, axis=1, keepdims=True), jnp.sum(hidden * hidden...]
    dot_general x9 -> x0, matrix products: 17 us -> none  [the longest x1 5.09 us: body(): jnp.dot(ctx, lax.all_gather(output_projection_weight, 'dp', axis=1, tiled...]
  transfers between devices with their start and end apart: 5 -> 0, of which waited for: 4 -> 0; matrix products, arithmetic and copies ran while one was open for 3% -> 0% of each run, Pallas kernels for 0% -> 0%
where the time goes in v2:
time: 89.1 us; the launch traced here: 88.7 us
  Pallas kernels  79.8 us (90%)
  local copies, waits for them, and re-layouts  8.24 us (9%)
    pallas_call x1, Pallas kernels, body(): pl.pallas_call(kernel, out_shape=(jax.ShapeDtypeStruct((10, RANK), F32),...  79.8 us
    unnamed x20, local copies, waits for them, and re-layouts  8.24 us

profile of v2, /device:TPU:1, one launch (start us, length us, event | category | flops | bytes accessed | tf_op | source)
XLA Modules:
  0.0 88.7 jit_solution(12306050631264852746)
XLA Ops:
  0.6 0.0 copy-start.7
  0.6 0.0 copy-start.8
  0.7 0.7 copy-done.7
  1.3 0.0 copy-done.8
  1.3 0.0 copy-start
  1.3 1.0 %copy-done = bf16[256,640]{1,0:T(8,128)(2,1)S(1)} copy-done((bf16[256,640]{1,0:T(8,128)(2,1)S(1)}, bf16[256,640]{1,0:T(8,128)(2,1)}, u32[]{:S(2)}) %copy-start) | copy-done | bytes 327704
  2.3 0.0 copy-start.1
  2.3 1.0 %copy-done.1 = bf16[256,640]{1,0:T(8,128)(2,1)S(1)} copy-done((bf16[256,640]{1,0:T(8,128)(2,1)S(1)}, bf16[256,640]{1,0:T(8,128)(2,1)}, u32[]{:S(2)}) %copy-start.1) | copy-done | bytes 327704
  3.3 0.0 copy-start.2
  3.3 0.9 %copy-done.2 = bf16[640,80]{0,1:T(8,128)(2,1)S(1)} copy-done((bf16[640,80]{0,1:T(8,128)(2,1)S(1)}, bf16[640,80]{0,1:T(8,128)(2,1)}, u32[]{:S(2)}) %copy-start.2) | copy-done | bytes 102424
  4.2 0.0 copy-start.3
  4.2 0.9 copy-done.3
  5.1 0.0 copy-start.4
  5.1 0.9 copy-done.4
  5.9 0.0 copy-start.5
  5.9 0.9 copy-done.5
  6.8 0.0 copy-start.6
  6.8 0.9 copy-done.6
  7.7 79.8 %hvp.1 = (f32[10,64]{1,0:T(8,128)S(1)}, f32[1,640]{1,0:T(1,128)S(1)}) custom-call(bf16[256,640]{1,0:T(8,128)(2,1)S(1)} %copy-done, bf16[256,640]{1,0:T(8,128)(2,1)S(1)} %copy-done.1, bf16[80,640]{1,0:T(8,128)(2,1)S(1)} %bitcast.4, bf16[64,640]{1,0:T(8,128)(2,1)S(1)} %bitcast.5, bf16[64,640]{1,0:T(8,128)(2,1)S(1)} %bitcast.6, bf16[64,640]{1,0:T(8,128)(2,1)S(1)} %copy-done.5, ...), custom_call_target="tpu_custom_call" | custom-call | flops 1677721600 | bytes 2097152 | tf_op jit(solution)/shard_map/hvp/pallas_call | solution.py:503
  87.5 0.6 copy.13
  88.1 0.6 copy.14
Async XLA Ops:
  0.6 0.7 copy-start.7
  0.6 0.7 copy-start.8
  1.3 1.0 %copy-start = (bf16[256,640]{1,0:T(8,128)(2,1)S(1)}, bf16[256,640]{1,0:T(8,128)(2,1)}, u32[]{:S(2)}) copy-start(bf16[256,640]{1,0:T(8,128)(2,1)} %ctx_ref.1) | copy-start | bytes 983044
  2.3 1.0 %copy-start.1 = (bf16[256,640]{1,0:T(8,128)(2,1)S(1)}, bf16[256,640]{1,0:T(8,128)(2,1)}, u32[]{:S(2)}) copy-start(bf16[256,640]{1,0:T(8,128)(2,1)} %resid_ref.1) | copy-start | bytes 983044
  3.3 0.9 %copy-start.2 = (bf16[640,80]{0,1:T(8,128)(2,1)S(1)}, bf16[640,80]{0,1:T(8,128)(2,1)}, u32[]{:S(2)}) copy-start(bf16[640,80]{0,1:T(8,128)(2,1)} %param.11) | copy-start | bytes 307204
  4.2 0.9 %copy-start.3 = (bf16[640,64]{0,1:T(8,128)(2,1)S(1)}, bf16[640,64]{0,1:T(8,128)(2,1)}, u32[]{:S(2)}) copy-start(bf16[640,64]{0,1:T(8,128)(2,1)} %param.12) | copy-start | bytes 245764
  5.1 0.9 %copy-start.4 = (bf16[640,64]{0,1:T(8,128)(2,1)S(1)}, bf16[640,64]{0,1:T(8,128)(2,1)}, u32[]{:S(2)}) copy-start(bf16[640,64]{0,1:T(8,128)(2,1)} %param.14) | copy-start | bytes 245764
  5.9 0.9 %copy-start.5 = (bf16[64,640]{1,0:T(8,128)(2,1)S(1)}, bf16[64,640]{1,0:T(8,128)(2,1)}, u32[]{:S(2)}) copy-start(bf16[64,640]{1,0:T(8,128)(2,1)} %b_ref.1) | copy-start | bytes 245764
  6.8 0.9 %copy-start.6 = (bf16[64,640]{1,0:T(8,128)(2,1)S(1)}, bf16[64,640]{1,0:T(8,128)(2,1)}, u32[]{:S(2)}) copy-start(bf16[64,640]{1,0:T(8,128)(2,1)} %u_ref.1) | copy-start | bytes 245764

commit v3 on v2

v3 whole, which is shorter than its diff:
```python
import functools

import jax
import jax.numpy as jnp
from jax import lax
from jax.experimental import pallas as pl
from jax.experimental.pallas import tpu as pltpu
from jax.sharding import Mesh, PartitionSpec as P

AXES = ("x", "z", "y", "c")
NX, NZ, NY, NC = 4, 16, 4, 2
SEQ = 128
RANK = 64
FEATS = 1280
HALF = 640
COLS = 80
TOKENS = 16384
WIDTH = 5120
BF = jnp.bfloat16
F32 = jnp.float32
CHUNKS = ((0, 1),) + tuple((2 * s - 1, 2 * s + 1) for s in range(1, 8)) + ((15, 16),)
PARTS = ((0, 32), (32, 32), (64, 16))
NP = len(PARTS)
NCH = len(CHUNKS)
NT = (((1,), (1,)), ((), ()))
TN = (((0,), (0,)), ((), ()))


def split2(v):
    hi = v.astype(BF)
    lo = (v - hi.astype(F32)).astype(BF)
    return hi, lo


def split3(v):
    hi = v.astype(BF)
    rest = v - hi.astype(F32)
    mid = rest.astype(BF)
    lo = (rest - mid.astype(F32)).astype(BF)
    return hi, mid, lo


def dot(a, b, dims=(((1,), (0,)), ((), ()))):
    return lax.dot_general(a, b, dims, preferred_element_type=F32)


def kernel(
    ctx_ref, resid_ref, wt_ref, at_ref, dt_ref, b_ref, u_ref, g_ref, len_ref,
    out_a, out_b,
    ctx_v, resid_v, bu_v, g_v, len_v,
    ctxs, ctxg, wg, adg, rt, relay, rrecv, buT, gr, part, rsb, zp, zr, zsum, zall, es, ls, h_ref, dh_ref, gh_ref,
    qg, ha_snd, ha_sib, hb_snd, hb_sib, hb_red, hb_rcv, ha_sum, hb2, hbz, ha2, haz,
    s_in, s_ctx, r_ctx, s_w, r_w, s_ws, r_ws, s_ad, r_ad, s_res, r_res, s_rel, r_rel, s_bu, r_bu, s_rs, r_rs,
    s_zr, r_zr, s_zd, r_zd, s_es, r_es, s_st, r_st, s_q, r_q, s_ha, r_ha, s_hs, r_hs, s_hb, r_hb, s_bz, r_bz, s_az, r_az,
):
    x, z, y, c = [lax.axis_index(a) for a in AXES]
    other = lax.rem(c + 1, NC)
    diag = x == y

    def mod4(v):
        return lax.rem(v + 8, 4)

    def dev(dx=0, dz=0, dy=0, dc=0):
        return (mod4(x + dx), lax.rem(z + dz + NZ, NZ), mod4(y + dy), lax.rem(c + dc, NC))

    def rcopy(src, dst, ss, rs, to):
        return pltpu.make_async_remote_copy(
            src_ref=src, dst_ref=dst, send_sem=ss, recv_sem=rs, device_id=to, device_id_type=pl.DeviceIdType.MESH
        )

    def arrived(dst, rs):
        rcopy(dst, dst, s_ad.at[0], rs, dev(0, 0, 0, 1)).wait_recv()

    pending = []

    def send(src, dst, ss, rs, to):
        cp = rcopy(src, dst, ss, rs, to)
        cp.start()
        pending.append((None, cp))

    def send_unless(cond, src, dst, ss, rs, to):
        cp = rcopy(src, dst, ss, rs, to)
        keep = jnp.logical_not(cond)

        @pl.when(keep)
        def _():
            cp.start()

        pending.append((keep, cp))

    loads = [
        pltpu.make_async_copy(src, dst, s_in.at[i])
        for i, (src, dst) in enumerate((
            (wt_ref, wg.at[c, 0]),
            (ctx_ref, ctx_v),
            (at_ref, adg.at[c, pl.ds(0, RANK)]),
            (dt_ref, adg.at[c, pl.ds(RANK, RANK)]),
            (resid_ref, resid_v),
            (b_ref, bu_v.at[pl.ds(0, RANK)]),
            (u_ref, bu_v.at[pl.ds(RANK, RANK)]),
            (g_ref, g_v),
            (len_ref, len_v),
        ))
    ]
    for cp in loads:
        cp.start()

    barrier = pltpu.get_barrier_semaphore()
    count = 0
    for dx in range(NX):
        for dy in range(NY):
            for dc in range(NC):
                if (dx, dy, dc) != (0, 0, 0):
                    pl.semaphore_signal(barrier, inc=1, device_id=dev(dx, 0, dy, dc), device_id_type=pl.DeviceIdType.MESH)
                    count += 1
    for dz in (-1, 1):
        pl.semaphore_signal(barrier, inc=1, device_id=dev(0, dz), device_id_type=pl.DeviceIdType.MESH)
        count += 1
    pl.semaphore_wait(barrier, count)

    def w_copy(s, flow, sub):
        if s == 8:
            src, dst = 13 + flow, 15
        else:
            src, dst = (0 if s == 1 else 2 * s - 3 + flow), 2 * s - 1 + flow
        rows = pl.ds(*PARTS[sub])
        k = NP * (2 * (s - 1) + flow) + sub
        source = wt_ref.at[rows] if s == 1 else wg.at[c, src, rows]
        return rcopy(source, wg.at[c, dst, rows], s_w.at[k], r_w.at[k], dev(0, 1 - 2 * flow))

    def w_start(s, flow, sub):
        cp = w_copy(s, flow, sub)
        cp.start()
        pending.append((None, cp))

    def w_sib(slot):
        send(wg.at[c, slot], wg.at[c, slot], s_ws.at[slot], r_ws.at[slot], dev(0, 0, 0, 1))

    def first(sub):
        for flow in range(2):
            w_start(1, flow, sub)

    first(0)
    loads[1].wait()
    for half in range(2):
        ctxs[half] = ctx_v[half * SEQ:(half + 1) * SEQ, :].T
    lead = 1 - 2 * c
    ctx_sends_to = lambda which, dx, k: [
        send(ctxs.at[half], ctxg.at[x, c], s_ctx.at[2 * which + half], r_ctx.at[k], (mod4(x + dx), z, y, half))
        for half in range(2)
    ]
    ctx_sends_to(0, lead, jnp.where(c == 0, 1, 4))
    send(ctxs.at[other], ctxg.at[x, c], s_ctx.at[4], r_ctx.at[0], dev(0, 0, 0, 1))
    loads[0].wait()
    w_sib(0)
    loads[2].wait()
    loads[3].wait()
    send(adg.at[c], adg.at[c], s_ad.at[0], r_ad.at[0], dev(0, 0, 0, 1))
    ctxg[x, c] = ctxs[c]

    loads[4].wait()
    loads[8].wait()
    lane = lax.broadcasted_iota(jnp.int32, (16, SEQ), 1)
    off = jnp.logical_not(diag)
    for half in range(2):
        rt[half, 0:HALF] = resid_v[half * SEQ:(half + 1) * SEQ, :].T
        rt[half, HALF:] = jnp.where(lane < len_v[half], 1.0, 0.0).astype(BF)

        @pl.when(jnp.logical_and(diag, c == half))
        def _():
            rrecv[c] = rt[half]

    send_unless(diag, rt.at[0], relay.at[y, c], s_res.at[0], r_res.at[y, c], (x, z, x, 0))
    send_unless(jnp.logical_or(off, c == 0), rt.at[0], rrecv.at[c], s_res.at[0], r_rel.at[c], (x, z, x, 0))
    first(1)
    for i in (5, 6, 7):
        loads[i].wait()

    @pl.when(diag)
    def _():
        buT[c] = bu_v[...].T
        gr[c] = jnp.concatenate([g_v[...], jnp.zeros((3, SEQ), F32)], axis=0)

    for dy in range(1, NY):
        send_unless(off, buT.at[c], buT.at[c], s_bu.at[dy - 1], r_bu.at[0], dev(0, 0, dy))
        send_unless(off, gr.at[c], gr.at[c], s_bu.at[dy + 2], r_bu.at[1], dev(0, 0, dy))

    first(2)
    def block(j):
        return mod4(x + j)

    def mm(js, k):
        lo, hi = CHUNKS[k]
        rows = (hi - lo) * COLS
        rhs = [jnp.concatenate([ctxg[block(j), cc] for j in js], axis=1) for cc in range(2)]
        lhs = [wg[cc, lo:hi].reshape(rows, HALF) for cc in range(2)]
        out = (dot(lhs[0], rhs[0]) + dot(lhs[1], rhs[1])).astype(BF)
        piece = pl.ds(lo * COLS, rows)
        for i, j in enumerate(js):
            part[j, piece] = out[:, i * SEQ:(i + 1) * SEQ]
            dest = mod4(x + j)
            send_unless(
                dest == y, part.at[j, piece], rsb.at[y, piece], s_rs.at[j, k], r_rs.at[mod4(dest - y), k], (x, z, dest, c)
            )

    def last_hop(flow):
        return (0, 2) if flow == 0 else (1,)

    def w_take(s, sub):
        for flow in range(2):
            if s < 8 or sub in last_hop(flow):
                w_copy(s, flow, sub).wait_recv()
                if s < 7 or (s == 7 and sub in last_hop(flow)):
                    w_start(s + 1, flow, sub)
        if sub == NP - 1:
            for slot in range(2 * s - 1, min(2 * s + 1, NZ)):
                w_sib(slot)

    def sib_wait(k):
        for slot in range(*CHUNKS[k]):
            arrived(wg.at[c, slot], r_ws.at[slot])

    def ctx_forward(i, dx_src, half_c, to_dx, sem):
        blk = ctxg.at[mod4(x + dx_src), half_c]
        send(blk, blk, s_ctx.at[sem], r_ctx.at[i], dev(to_dx))

    def ctx_wait(i):
        arrived(ctxg.at[0, 0], r_ctx.at[i])

    def low_rank_sum():
        acc = zp[pl.ds(pl.multiple_of(y * 32, 32), 32)]
        for dy in range(1, NY):
            arrived(zr.at[dy], r_zr.at[dy])
            acc = acc + zr[dy]
        zsum[...] = acc
        for dq in range(NX):
            me = jnp.logical_and(diag, dq == 0)
            send_unless(me, zsum, zall.at[y], s_zd.at[dq], r_zd.at[y], (mod4(x + dq), z, x, c))

        @pl.when(diag)
        def _():
            zall[y] = acc

    def resid_half():
        send_unless(jnp.logical_and(diag, c == 1), rt.at[1], rrecv.at[c], s_res.at[1], r_rel.at[c], (y, z, x, 1))

    def second_leg():
        pass_on = jnp.logical_and(diag, c == 0)
        for dq in range(1, NX):
            q = mod4(x + dq)
            for cc in range(2):
                @pl.when(pass_on)
                def _():
                    arrived(relay.at[q, cc], r_res.at[q, cc])

                send_unless(
                    jnp.logical_not(pass_on), relay.at[q, cc], rrecv.at[cc], s_rel.at[dq, cc], r_rel.at[cc], (q, z, x, 0)
                )

    def adapter_on():
        @pl.when(off)
        def _():
            arrived(buT.at[c], r_bu.at[0])
            arrived(gr.at[c], r_bu.at[1])

        send(buT.at[c], buT.at[c], s_bu.at[6], r_bu.at[2], dev(0, 0, 0, 1))
        send(gr.at[c], gr.at[c], s_bu.at[7], r_bu.at[3], dev(0, 0, 0, 1))

    def hop(s, *work):
        for sub in range(NP):
            w_take(s, sub)
            for f in work[len(work) * sub // NP:len(work) * (sub + 1) // NP]:
                f()

    def zp_sum():
        ctx_wait(0)
        arrived(adg.at[c], r_ad.at[0])
        zp[...] = dot(adg[0], ctxg[x, 0]) + dot(adg[1], ctxg[x, 1])

    def zp_send():
        for dy in range(1, NY):
            rows = pl.ds(pl.multiple_of(mod4(y + dy) * 32, 32), 32)
            send(zp.at[rows], zr.at[dy], s_zr.at[dy], r_zr.at[dy], dev(0, 0, dy))

    def ctx_near():
        ctx_wait(2)
        ctx_wait(3)

    def ctx_pass():
        ctx_wait(1)
        ctx_forward(5, -1, 0, 1, 5)
        ctx_wait(4)
        ctx_forward(6, 1, 1, -1, 6)

    def ctx_far():
        ctx_wait(5)
        ctx_wait(6)

    def m(js, *ks):
        return lambda: [mm(js, k) for k in ks]

    def sw(k):
        return lambda: sib_wait(k)

    ctx_second = lambda: ctx_sends_to(1, -lead, jnp.where(c == 0, 3, 2))

    def low_rank_terms():
        for ys in range(NY):
            @pl.when(jnp.logical_not(jnp.logical_and(diag, y == ys)))
            def _():
                arrived(zall.at[ys], r_zd.at[ys])

        arrived(buT.at[c], r_bu.at[2])
        arrived(gr.at[c], r_bu.at[3])
        zt = jnp.concatenate([zall[0], zall[1]], axis=0)
        ztt = jnp.concatenate([zall[2], zall[3]], axis=0)
        zero = jnp.zeros((RANK, SEQ), F32)
        rhs = jnp.concatenate([jnp.concatenate([ztt, zt], axis=0), jnp.concatenate([zt, zero], axis=0)], axis=1)
        r1, r2, r3 = split3(rhs)
        for cc in range(2):
            b = buT[cc]
            both = dot(b, r1) + dot(b, r2) + dot(b, r3)
            dh_ref[cc * HALF:(cc + 1) * HALF] = both[:, 0:SEQ]
            h_ref[cc * HALF:(cc + 1) * HALF] = both[:, SEQ:]

    def fold(v):
        return jnp.sum(v.reshape(-1, 8, SEQ), axis=0)

    def early_sums():
        for i in range(10):
            col = jnp.broadcast_to(gr[i // 5, pl.ds(i % 5, 1)], (SEQ, SEQ)).T
            gh_ref[i * SEQ:(i + 1) * SEQ] = col * col
        acc = jnp.zeros((SEQ, 3 * SEQ), F32)
        sums = [jnp.zeros((8, SEQ), F32) for _ in range(3)]
        lane = lax.broadcasted_iota(jnp.int32, (HALF, SEQ), 1)
        for cc in range(2):
            rows = pl.ds(cc * HALF, HALF)
            g2 = gh_ref[rows]
            d = dh_ref[rows]
            gd = g2 * d
            d1, d2 = split2(gd)
            k1, k2 = split2(jnp.where(lane < RANK, 1.0, g2))
            acc = acc + dot(buT[cc], jnp.concatenate([d1, d2, k1], axis=1), TN)
            e2 = dot(buT[cc], k2, TN)
            acc = acc + jnp.concatenate([jnp.zeros((SEQ, 2 * SEQ), F32), e2], axis=1)
            sums = [s + fold(t) for s, t in zip(sums, (d, gd, g2))]
        es[0, 0:RANK] = acc[0:RANK, 0:SEQ] + acc[0:RANK, SEQ:2 * SEQ]
        es[0, RANK:2 * RANK] = acc[0:RANK, 2 * SEQ:]
        for n, s in enumerate(sums):
            es[0, 2 * RANK + n:2 * RANK + n + 1] = jnp.sum(s, axis=0, keepdims=True)
        es[0, 2 * RANK + 3:] = jnp.zeros((5, SEQ), F32)

    def early_send():
        for dx in range(1, NX):
            send(es.at[0], es.at[dx], s_es.at[dx], r_es.at[dx], (mod4(x + dx), z, y, c))

    hop(1, ctx_second, zp_sum, zp_send)
    hop(2, sw(0), m((0,), 0), lambda: None)
    hop(3, sw(1), m((0,), 1), ctx_pass)
    hop(4, sw(2), m((0,), 2), ctx_near, m((1, 3), 0), m((1, 3), 1), lambda: (low_rank_sum(), resid_half()))
    hop(5, m((1, 3), 2), sw(3), m((1, 3), 3), m((0,), 3), lambda: None, adapter_on)
    hop(6, sw(4), m((1, 3), 4), m((0,), 4), second_leg, ctx_far, m((2,), 0))
    hop(7, m((2,), 1, 2), m((2,), 3), sw(5), m((1, 3), 5), m((0,), 5), m((2,), 4, 5))
    hop(8, low_rank_terms, sw(6), m((1, 2), 6), m((0, 3), 6), early_sums, early_send)
    sib_wait(7)
    mm((0, 1, 2, 3), 7)
    sib_wait(8)
    mm((0, 1, 2, 3), 8)

    for cc in range(2):
        @pl.when(jnp.logical_not(jnp.logical_and(diag, c == cc)))
        def _():
            arrived(rrecv.at[cc], r_rel.at[cc])
        h_ref[cc * HALF:(cc + 1) * HALF] = h_ref[cc * HALF:(cc + 1) * HALF] + rrecv[cc, 0:HALF].astype(F32)
    live = rrecv[0, HALF:].astype(F32)[0:1] * (1.0 / jnp.sqrt(jnp.float32(TOKENS)))

    jown = mod4(y - x)
    for k, (lo, hi) in enumerate(CHUNKS):
        for dy in range(1, NY):
            piece = pl.ds(lo * COLS, (hi - lo) * COLS)
            arrived(rsb.at[mod4(y - dy), piece], r_rs.at[dy, k])
        for slot in range(lo, hi):
            step = (slot + 1) // 2
            zz = z if slot == 0 else (z - step if slot % 2 == 1 else z + step)
            zz = lax.rem(zz + NZ, NZ)
            rows = pl.ds(pl.multiple_of(zz * COLS, 16), COLS)
            piece = pl.ds(slot * COLS, COLS)
            acc = part[jown, piece].astype(F32)
            for dy in range(1, NY):
                acc = acc + rsb[mod4(y - dy), piece].astype(F32)
            h_ref[rows] = h_ref[rows] + acc

    acc = jnp.zeros((SEQ, 4 * SEQ), F32)
    sums = [jnp.zeros((8, SEQ), F32) for _ in range(6)]
    for cc in range(2):
        rows = pl.ds(cc * HALF, HALF)
        h = h_ref[rows]
        d = dh_ref[rows]
        g2 = gh_ref[rows]
        gh = g2 * h
        h1, h2 = split2(h)
        g1, g3 = split2(gh)
        acc = acc + dot(buT[cc], jnp.concatenate([h1, h2, g1, g3], axis=1), TN)
        sums = [s + fold(t) for s, t in zip(sums, (h, h * h, h * d, gh, gh * h, gh * d))]
    ls[0, 0:RANK] = acc[0:RANK, 0:SEQ] + acc[0:RANK, SEQ:2 * SEQ]
    ls[0, RANK:2 * RANK] = acc[0:RANK, 2 * SEQ:3 * SEQ] + acc[0:RANK, 3 * SEQ:]
    for n, s in enumerate(sums):
        ls[0, 2 * RANK + n:2 * RANK + n + 1] = jnp.sum(s, axis=0, keepdims=True)
    ls[0, 2 * RANK + 6:] = jnp.zeros((2, SEQ), F32)
    for dx in range(1, NX):
        send(ls.at[0], ls.at[dx], s_st.at[dx], r_st.at[dx], (mod4(x + dx), z, y, c))
    early = es[0]
    for dx in range(1, NX):
        arrived(es.at[dx], r_es.at[dx])
        early = early + es[dx]
    late = ls[0]
    for dx in range(1, NX):
        arrived(ls.at[dx], r_st.at[dx])
        late = late + ls[dx]
    inv = 1.0 / WIDTH
    m1, e_gd, e_g = [early[2 * RANK + n:2 * RANK + n + 1] * inv for n in range(3)]
    mu, e_hh, e_hd, e_gh, e_ghh, e_ghd = [late[2 * RANK + n:2 * RANK + n + 1] * inv for n in range(6)]
    rinv = lax.rsqrt(e_hh - mu * mu + 1e-05)
    m2 = rinv * (e_hd - mu * m1)
    g_n = rinv * (e_gh - mu * e_g)
    g_nn = rinv * rinv * (e_ghh - 2.0 * mu * e_gh + mu * mu * e_g)
    g_nd = rinv * (e_ghd - mu * e_gd)
    lr = live * rinv
    m3 = lr * (e_gd - m1 * e_g - m2 * g_n)
    m4 = lr * (g_nd - m1 * g_n - m2 * g_nn)
    b_one = jnp.broadcast_to(early[RANK:2 * RANK, 0:1], (RANK, SEQ))
    b_g = jnp.broadcast_to(early[RANK:2 * RANK, SEQ - 1:SEQ], (RANK, SEQ))
    b_n = rinv * (late[0:RANK] - mu * b_one)
    b_gn = rinv * (late[RANK:2 * RANK] - mu * b_g)
    b_c = lr * (early[0:RANK] - m1 * b_g - m2 * b_gn)
    q1, q2 = split2(rinv * (b_c - m3 * b_one - m4 * b_n))
    xq = y
    qg[xq] = jnp.concatenate([q1, q2], axis=0).T
    for dy in range(1, NY):
        send(qg.at[xq], qg.at[xq], s_q.at[dy], r_q.at[dy], dev(0, 0, dy))

    z1, z2 = split2(jnp.concatenate([zall[0], zall[1]], axis=0))
    zs = jnp.concatenate([z1, z2], axis=0)
    for cc in range(2):
        rows = pl.ds(cc * HALF, HALF)
        n = (h_ref[rows] - mu) * rinv
        cot = lr * gh_ref[rows] * (dh_ref[rows] - m1 - n * m2)
        g1, g2 = split2(rinv * (cot - m3 - n * m4))
        hb = dot(zs, g1, NT) + dot(zs, g2, NT)
        hb = hb[0:RANK] + hb[RANK:]
        for p in range(NX):
            hb_snd[cc, p] = hb[16 * p:16 * (p + 1)]
    send(hb_snd.at[other], hb_sib, s_hs.at[0], r_hs.at[0], dev(0, 0, 0, 1))
    arrived(hb_sib, r_hs.at[0])
    hb_red[...] = hb_snd[c] + hb_sib[...]
    for dp in range(NX):
        p = mod4(x + dp)
        me = jnp.logical_and(diag, dp == 0)
        send_unless(me, hb_red.at[p], hb_rcv.at[y], s_hb.at[dp], r_hb.at[y], (p, z, x, c))

    @pl.when(diag)
    def _():
        hb_rcv[y] = hb_red[x]

    for dy in range(1, NY):
        arrived(qg.at[xq], r_q.at[dy])
    qs = jnp.concatenate([qg[xb] for xb in range(NX)], axis=0)
    mine = pl.ds(pl.multiple_of(x * 160, 32), 160)
    for cc in range(2):
        t = dot(jnp.concatenate([ctxg[xb, cc, mine] for xb in range(NX)], axis=1), qs)
        ha_snd[cc] = t + pltpu.roll(t, RANK, 1)
    send(ha_snd.at[other], ha_sib, s_ha.at[0], r_ha.at[0], dev(0, 0, 0, 1))
    arrived(ha_sib, r_ha.at[0])
    ha_sum[...] = ha_snd[c] + ha_sib[...]
    low = lax.broadcasted_iota(jnp.int32, (NZ, SEQ), 1) < RANK
    pairs = []
    for k in range(5):
        pairs.append(jnp.where(low, ha_sum[pl.ds(2 * k, NZ, stride=10)], ha_sum[pl.ds(2 * k + 1, NZ, stride=10)]))
    v = jnp.concatenate(pairs, axis=1)
    for zi in range(NZ):
        ha2[zi] = v[zi:zi + 1]
    for dz in range(1, NZ):
        send(ha2.at[lax.rem(z + dz, NZ)], haz.at[dz], s_az.at[dz], r_az.at[dz], dev(0, dz))
    for ys in range(NY):
        @pl.when(jnp.logical_not(jnp.logical_and(diag, y == ys)))
        def _():
            arrived(hb_rcv.at[ys], r_hb.at[ys])
    acc = hb_rcv[0] + hb_rcv[1] + hb_rcv[2] + hb_rcv[3]
    for zi in range(NZ):
        hb2[zi] = acc[zi:zi + 1]
    for dz in range(1, NZ):
        send(hb2.at[lax.rem(z + dz, NZ)], hbz.at[dz], s_bz.at[dz], r_bz.at[dz], dev(0, dz))
    acc = ha2[z]
    for dz in range(1, NZ):
        arrived(haz.at[dz], r_az.at[dz])
        acc = acc + haz[dz]
    for k in range(10):
        out_a[k:k + 1] = acc[:, k * RANK:(k + 1) * RANK]
    acc = hb2[z]
    for dz in range(1, NZ):
        arrived(hbz.at[dz], r_bz.at[dz])
        acc = acc + hbz[dz]
    out_b[...] = acc

    for keep, cp in pending:
        if keep is None:
            cp.wait_send()
        else:
            @pl.when(keep)
            def _():
                cp.wait_send()


def body(ctx, resid, w, a, b, d, u, gain, lengths):
    vmem = pl.BlockSpec(memory_space=pltpu.VMEM)
    dma = lambda *n: pltpu.SemaphoreType.DMA(n)
    return pl.pallas_call(
        kernel,
        out_shape=(jax.ShapeDtypeStruct((10, RANK), F32), jax.ShapeDtypeStruct((1, HALF), F32)),
        in_specs=[pl.BlockSpec(memory_space=pltpu.HBM)] * 9,
        out_specs=(vmem, vmem),
        scratch_shapes=[
            pltpu.VMEM((2 * SEQ, HALF), BF),
            pltpu.VMEM((2 * SEQ, HALF), BF),
            pltpu.VMEM((2 * RANK, HALF), BF),
            pltpu.VMEM((5, SEQ), F32),
            pltpu.SMEM((2,), jnp.int32),
            pltpu.VMEM((2, HALF, SEQ), BF),
            pltpu.VMEM((NX, NC, HALF, SEQ), BF),
            pltpu.VMEM((NC, NZ, COLS, HALF), BF),
            pltpu.VMEM((NC, 2 * RANK, HALF), BF),
            pltpu.VMEM((2, HALF + 16, SEQ), BF),
            pltpu.VMEM((NX, 2, HALF + 16, SEQ), BF),
            pltpu.VMEM((2, HALF + 16, SEQ), BF),
            pltpu.VMEM((NC, HALF, SEQ), BF),
            pltpu.VMEM((NC, 8, SEQ), F32),
            pltpu.VMEM((NX, FEATS, SEQ), BF),
            pltpu.VMEM((NY, FEATS, SEQ), BF),
            pltpu.VMEM((SEQ, SEQ), F32),
            pltpu.VMEM((NY, 32, SEQ), F32),
            pltpu.VMEM((32, SEQ), F32),
            pltpu.VMEM((NY, 32, SEQ), F32),
            pltpu.VMEM((NX, 2 * RANK + 8, SEQ), F32),
            pltpu.VMEM((NX, 2 * RANK + 8, SEQ), F32),
            pltpu.VMEM((FEATS, SEQ), F32),
            pltpu.VMEM((FEATS, SEQ), F32),
            pltpu.VMEM((FEATS, SEQ), F32),
            pltpu.VMEM((NX, SEQ, SEQ), BF),
            pltpu.VMEM((NC, 160, SEQ), F32),
            pltpu.VMEM((160, SEQ), F32),
            pltpu.VMEM((NC, NX, 16, HALF), F32),
            pltpu.VMEM((NX, 16, HALF), F32),
            pltpu.VMEM((NX, 16, HALF), F32),
            pltpu.VMEM((NY, 16, HALF), F32),
            pltpu.VMEM((160, SEQ), F32),
            pltpu.VMEM((NZ, 1, HALF), F32),
            pltpu.VMEM((NZ, 1, HALF), F32),
            pltpu.VMEM((NZ, 1, HALF), F32),
            pltpu.VMEM((NZ, 1, HALF), F32),
            dma(9),
            dma(7), dma(7), dma(16 * NP), dma(16 * NP), dma(16), dma(16), dma(1), dma(1), dma(2), dma(NX, 2), dma(NX, 2), dma(2),
            dma(8), dma(4), dma(NX, NCH), dma(NY, NCH),
            dma(NY), dma(NY), dma(NX), dma(NY), dma(NX), dma(NX), dma(NX), dma(NX), dma(NY), dma(NY), dma(1), dma(1),
            dma(1), dma(1),
            dma(NX), dma(NY), dma(NZ), dma(NZ), dma(NZ), dma(NZ),
        ],
        compiler_params=pltpu.CompilerParams(collective_id=0, has_side_effects=True, vmem_limit_bytes=60 << 20),
        cost_estimate=pl.CostEstimate(flops=2 * 1280 * 1280 * 512, bytes_accessed=2 << 20, transcendentals=0),
        name="hvp",
    )(ctx, resid, w.T, a.T, d.T, b, u, gain.reshape(5, SEQ), lengths)


def solution(mesh):
    grid = Mesh(mesh.devices.reshape(NX, NZ, NY, NC), AXES)
    dp, tensor = ("x", "z"), ("y", "c")
    in_specs = (
        P(dp, tensor),
        P(dp, tensor),
        P(tensor, dp),
        P(tensor, None),
        P(None, tensor),
        P(tensor, None),
        P(None, tensor),
        P(tensor),
        P(dp),
    )
    out_specs = (P(("y", "c", "x", "z"), None), P(dp, tensor))
    return jax.shard_map(body, mesh=grid, in_specs=in_specs, out_specs=out_specs, check_vma=False)
```

time: 89.1 us -> 78.5 us (0.88)
  local copies, waits for them, and re-layouts: 8.24 us -> 1.88 us
  Pallas kernels: 79.8 us -> 75.2 us
    unnamed x20 -> x4, local copies, waits for them, and re-layouts: 8.24 us -> 1.88 us
    pallas_call x1, Pallas kernels: 79.8 us -> 75.2 us  [body(): pl.pallas_call(kernel, out_shape=(jax.ShapeDtypeStruct((10, RANK), F32),...]
where the time goes in v3:
time: 78.5 us; the launch traced here: 77.7 us
  Pallas kernels  75.2 us (96%)
  local copies, waits for them, and re-layouts  1.88 us (2%)
    pallas_call x1, Pallas kernels, body(): pl.pallas_call(kernel, out_shape=(jax.ShapeDtypeStruct((10, RANK), F32),...  75.2 us
    unnamed x4, local copies, waits for them, and re-layouts  1.88 us

profile of v3, /device:TPU:1, one launch (start us, length us, event | category | flops | bytes accessed | tf_op | source)
XLA Modules:
  0.0 77.7 jit_solution(16048326427396145885)
XLA Ops:
  0.6 75.2 %hvp.1 = (f32[10,64]{1,0:T(8,128)}, f32[1,640]{1,0:T(1,128)}) custom-call(bf16[256,640]{1,0:T(8,128)(2,1)} %ctx_ref.1, bf16[256,640]{1,0:T(8,128)(2,1)} %resid_ref.1, bf16[80,640]{1,0:T(8,128)(2,1)} %bitcast.4, bf16[64,640]{1,0:T(8,128)(2,1)} %bitcast.5, bf16[64,640]{1,0:T(8,128)(2,1)} %bitcast.6, bf16[64,640]{1,0:T(8,128)(2,1)} %b_ref.1, ...), custom_call_target="tpu_custom_call" | custom-call | flops 1677721600 | bytes 2097152 | tf_op jit(solution)/shard_map/hvp/pallas_call | solution.py:517
  75.8 0.0 copy-start
  75.8 1.3 %copy.13 = f32[10,64]{1,0:T(8,128)} copy(f32[10,64]{1,0:T(8,128)} %get-tuple-element.4) | data formatting | bytes 5120
  77.1 0.0 copy-done
  77.1 0.6 copy.14
Async XLA Ops:
  75.8 1.3 %copy-start = (f32[1,640]{1,0:T(1,128)S(1)}, f32[1,640]{1,0:T(1,128)}, u32[]{:S(2)}) copy-start(f32[1,640]{1,0:T(1,128)} %get-tuple-element.5) | copy-start | bytes 7684

commit v4 on v3

--- a/solution.py
+++ b/solution.py
@@ -18,8 +18,8 @@
 WIDTH = 5120
 BF = jnp.bfloat16
 F32 = jnp.float32
-CHUNKS = ((0, 1),) + tuple((2 * s - 1, 2 * s + 1) for s in range(1, 8)) + ((15, 16),)
-PARTS = ((0, 32), (32, 32), (64, 16))
+CHUNKS = ((0, 1),) + tuple((2 * s - 1, 2 * s + 1) for s in range(1, 7)) + ((13, 16),)
+PARTS = tuple((16 * i, 16) for i in range(5))
 NP = len(PARTS)
 NCH = len(CHUNKS)
 NT = (((1,), (1,)), ((), ()))
@@ -48,10 +48,10 @@
     ctx_ref, resid_ref, wt_ref, at_ref, dt_ref, b_ref, u_ref, g_ref, len_ref,
     out_a, out_b,
     ctx_v, resid_v, bu_v, g_v, len_v,
-    ctxs, ctxg, wg, adg, rt, relay, rrecv, buT, gr, part, rsb, zp, zr, zsum, zall, es, ls, h_ref, dh_ref, gh_ref,
-    qg, ha_snd, ha_sib, hb_snd, hb_sib, hb_red, hb_rcv, ha_sum, hb2, hbz, ha2, haz,
+    ctxs, ctxg, wg, adg, rt, relay, rrecv, buT, gr, part, rsb, zp, zr, zsum, zall, es, ts, ls, h_ref, dh_ref, gh_ref,
+    qg, ha_snd, ha_sib, hb_snd, hb_sib, hb_red, hb_rcv, ha_sum, ab, abz,
     s_in, s_ctx, r_ctx, s_w, r_w, s_ws, r_ws, s_ad, r_ad, s_res, r_res, s_rel, r_rel, s_bu, r_bu, s_rs, r_rs,
-    s_zr, r_zr, s_zd, r_zd, s_es, r_es, s_st, r_st, s_q, r_q, s_ha, r_ha, s_hs, r_hs, s_hb, r_hb, s_bz, r_bz, s_az, r_az,
+    s_zr, r_zr, s_zd, r_zd, s_es, r_es, s_ts, r_ts, s_st, r_st, s_q, r_q, s_ha, r_ha, s_hs, r_hs, s_hb, r_hb, s_ab, r_ab,
 ):
     x, z, y, c = [lax.axis_index(a) for a in AXES]
     other = lax.rem(c + 1, NC)
@@ -71,22 +71,22 @@
     def arrived(dst, rs):
         rcopy(dst, dst, s_ad.at[0], rs, dev(0, 0, 0, 1)).wait_recv()
 
-    pending = []
+    def left(src, ss):
+        rcopy(src, src, ss, r_ad.at[0], dev(0, 0, 0, 1)).wait_send()
 
     def send(src, dst, ss, rs, to):
-        cp = rcopy(src, dst, ss, rs, to)
-        cp.start()
-        pending.append((None, cp))
+        rcopy(src, dst, ss, rs, to).start()
 
     def send_unless(cond, src, dst, ss, rs, to):
-        cp = rcopy(src, dst, ss, rs, to)
-        keep = jnp.logical_not(cond)
-
-        @pl.when(keep)
-        def _():
-            cp.start()
-
-        pending.append((keep, cp))
+        @pl.when(jnp.logical_not(cond))
+        def _():
+            send(src, dst, ss, rs, to)
+
+    def first_three(ref):
+        return ref.at[pl.ds(0, 3)]
+
+    def last_three(ref):
+        return ref.at[pl.ds(1, 3)]
 
     loads = [
         pltpu.make_async_copy(src, dst, s_in.at[i])
@@ -106,35 +106,30 @@
         cp.start()
 
     barrier = pltpu.get_barrier_semaphore()
-    count = 0
-    for dx in range(NX):
-        for dy in range(NY):
-            for dc in range(NC):
-                if (dx, dy, dc) != (0, 0, 0):
-                    pl.semaphore_signal(barrier, inc=1, device_id=dev(dx, 0, dy, dc), device_id_type=pl.DeviceIdType.MESH)
-                    count += 1
-    for dz in (-1, 1):
-        pl.semaphore_signal(barrier, inc=1, device_id=dev(0, dz), device_id_type=pl.DeviceIdType.MESH)
-        count += 1
+    first_partners = [dev(0, dz) for dz in (-1, 1)]
+    first_partners += [dev(dx, 0, 0, dc) for dx in (1, 3, 2) for dc in range(NC)]
+    first_partners += [dev(0, 0, dy, dc) for dy in (1, 3, 2) for dc in range(NC)]
+    first_partners += [dev(0, 0, 0, 1)]
+    for partner in first_partners:
+        pl.semaphore_signal(barrier, inc=1, device_id=partner, device_id_type=pl.DeviceIdType.MESH)
+    count = len(first_partners)
     pl.semaphore_wait(barrier, count)
 
     def w_copy(s, flow, sub):
         if s == 8:
-            src, dst = 13 + flow, 15
+            src, dst = 11 + flow, 15
         else:
             src, dst = (0 if s == 1 else 2 * s - 3 + flow), 2 * s - 1 + flow
         rows = pl.ds(*PARTS[sub])
-        k = NP * (2 * (s - 1) + flow) + sub
         source = wt_ref.at[rows] if s == 1 else wg.at[c, src, rows]
-        return rcopy(source, wg.at[c, dst, rows], s_w.at[k], r_w.at[k], dev(0, 1 - 2 * flow))
+        return rcopy(source, wg.at[c, dst, rows], s_w.at[0], r_w.at[NP * (s - 1) + sub], dev(0, (1 - 2 * flow) * (2 if s == 8 else 1)))
 
     def w_start(s, flow, sub):
-        cp = w_copy(s, flow, sub)
-        cp.start()
-        pending.append((None, cp))
+        w_copy(s, flow, sub).start()
 
     def w_sib(slot):
-        send(wg.at[c, slot], wg.at[c, slot], s_ws.at[slot], r_ws.at[slot], dev(0, 0, 0, 1))
+        k = min((slot + 1) // 2, 7)
+        send(wg.at[c, slot], wg.at[c, slot], s_ws.at[0], r_ws.at[k], dev(0, 0, 0, 1))
 
     def first(sub):
         for flow in range(2):
@@ -145,12 +140,12 @@
     for half in range(2):
         ctxs[half] = ctx_v[half * SEQ:(half + 1) * SEQ, :].T
     lead = 1 - 2 * c
-    ctx_sends_to = lambda which, dx, k: [
-        send(ctxs.at[half], ctxg.at[x, c], s_ctx.at[2 * which + half], r_ctx.at[k], (mod4(x + dx), z, y, half))
+    ctx_sends_to = lambda dx, k: [
+        send(ctxs.at[half], ctxg.at[x, c], s_ctx.at[0], r_ctx.at[k], (mod4(x + dx), z, y, half))
         for half in range(2)
     ]
-    ctx_sends_to(0, lead, jnp.where(c == 0, 1, 4))
-    send(ctxs.at[other], ctxg.at[x, c], s_ctx.at[4], r_ctx.at[0], dev(0, 0, 0, 1))
+    ctx_sends_to(lead, jnp.where(c == 0, 1, 4))
+    send(ctxs.at[other], ctxg.at[x, c], s_ctx.at[1], r_ctx.at[0], dev(0, 0, 0, 1))
     loads[0].wait()
     w_sib(0)
     loads[2].wait()
@@ -170,9 +165,10 @@
         def _():
             rrecv[c] = rt[half]
 
-    send_unless(diag, rt.at[0], relay.at[y, c], s_res.at[0], r_res.at[y, c], (x, z, x, 0))
+    send_unless(diag, rt.at[0], relay.at[y, c], s_res.at[0], r_res.at[0], (x, z, x, 0))
     send_unless(jnp.logical_or(off, c == 0), rt.at[0], rrecv.at[c], s_res.at[0], r_rel.at[c], (x, z, x, 0))
     first(1)
+    first(2)
     for i in (5, 6, 7):
         loads[i].wait()
 
@@ -182,10 +178,11 @@
         gr[c] = jnp.concatenate([g_v[...], jnp.zeros((3, SEQ), F32)], axis=0)
 
     for dy in range(1, NY):
-        send_unless(off, buT.at[c], buT.at[c], s_bu.at[dy - 1], r_bu.at[0], dev(0, 0, dy))
-        send_unless(off, gr.at[c], gr.at[c], s_bu.at[dy + 2], r_bu.at[1], dev(0, 0, dy))
-
-    first(2)
+        send_unless(off, buT.at[c], buT.at[c], s_bu.at[0], r_bu.at[0], dev(0, 0, dy))
+        send_unless(off, gr.at[c], gr.at[c], s_bu.at[1], r_bu.at[1], dev(0, 0, dy))
+
+    first(3)
+    first(4)
     def block(j):
         return mod4(x + j)
 
@@ -200,42 +197,44 @@
             part[j, piece] = out[:, i * SEQ:(i + 1) * SEQ]
             dest = mod4(x + j)
             send_unless(
-                dest == y, part.at[j, piece], rsb.at[y, piece], s_rs.at[j, k], r_rs.at[mod4(dest - y), k], (x, z, dest, c)
+                dest == y, part.at[j, piece], rsb.at[y, piece], s_rs.at[0], r_rs.at[k // (NCH - 1)], (x, z, dest, c)
             )
 
     def last_hop(flow):
-        return (0, 2) if flow == 0 else (1,)
+        return (0, 2, 4) if flow == 0 else (1, 3)
 
     def w_take(s, sub):
+        rows = pl.ds(*PARTS[sub])
+        arrived(wg.at[0, 0, rows] if s == 8 else wg.at[pl.ds(0, 2), 0, rows], r_w.at[NP * (s - 1) + sub])
         for flow in range(2):
-            if s < 8 or sub in last_hop(flow):
-                w_copy(s, flow, sub).wait_recv()
-                if s < 7 or (s == 7 and sub in last_hop(flow)):
-                    w_start(s + 1, flow, sub)
+            if s < 7:
+                w_start(s + 1, flow, sub)
+            if s == 6 and sub in last_hop(flow):
+                w_start(8, flow, sub)
         if sub == NP - 1:
             for slot in range(2 * s - 1, min(2 * s + 1, NZ)):
                 w_sib(slot)
 
     def sib_wait(k):
-        for slot in range(*CHUNKS[k]):
-            arrived(wg.at[c, slot], r_ws.at[slot])
-
-    def ctx_forward(i, dx_src, half_c, to_dx, sem):
+        lo, hi = CHUNKS[k]
+        arrived(wg.at[c, pl.ds(lo, hi - lo)], r_ws.at[k])
+
+    def ctx_forward(i, dx_src, half_c, to_dx):
         blk = ctxg.at[mod4(x + dx_src), half_c]
-        send(blk, blk, s_ctx.at[sem], r_ctx.at[i], dev(to_dx))
+        send(blk, blk, s_ctx.at[0], r_ctx.at[i], dev(to_dx))
 
     def ctx_wait(i):
         arrived(ctxg.at[0, 0], r_ctx.at[i])
 
     def low_rank_sum():
         acc = zp[pl.ds(pl.multiple_of(y * 32, 32), 32)]
+        arrived(last_three(zr), r_zr.at[0])
         for dy in range(1, NY):
-            arrived(zr.at[dy], r_zr.at[dy])
             acc = acc + zr[dy]
         zsum[...] = acc
         for dq in range(NX):
             me = jnp.logical_and(diag, dq == 0)
-            send_unless(me, zsum, zall.at[y], s_zd.at[dq], r_zd.at[y], (mod4(x + dq), z, x, c))
+            send_unless(me, zsum, zall.at[y], s_zd.at[0], r_zd.at[0], (mod4(x + dq), z, x, c))
 
         @pl.when(diag)
         def _():
@@ -246,15 +245,16 @@
 
     def second_leg():
         pass_on = jnp.logical_and(diag, c == 0)
+
+        @pl.when(pass_on)
+        def _():
+            arrived(first_three(relay), r_res.at[0])
+
         for dq in range(1, NX):
             q = mod4(x + dq)
             for cc in range(2):
-                @pl.when(pass_on)
-                def _():
-                    arrived(relay.at[q, cc], r_res.at[q, cc])
-
                 send_unless(
-                    jnp.logical_not(pass_on), relay.at[q, cc], rrecv.at[cc], s_rel.at[dq, cc], r_rel.at[cc], (q, z, x, 0)
+                    jnp.logical_not(pass_on), relay.at[q, cc], rrecv.at[cc], s_rel.at[0], r_rel.at[cc], (q, z, x, 0)
                 )
 
     def adapter_on():
@@ -263,8 +263,8 @@
             arrived(buT.at[c], r_bu.at[0])
             arrived(gr.at[c], r_bu.at[1])
 
-        send(buT.at[c], buT.at[c], s_bu.at[6], r_bu.at[2], dev(0, 0, 0, 1))
-        send(gr.at[c], gr.at[c], s_bu.at[7], r_bu.at[3], dev(0, 0, 0, 1))
+        send(buT.at[c], buT.at[c], s_bu.at[2], r_bu.at[2], dev(0, 0, 0, 1))
+        send(gr.at[c], gr.at[c], s_bu.at[3], r_bu.at[3], dev(0, 0, 0, 1))
 
     def hop(s, *work):
         for sub in range(NP):
@@ -280,7 +280,7 @@
     def zp_send():
         for dy in range(1, NY):
             rows = pl.ds(pl.multiple_of(mod4(y + dy) * 32, 32), 32)
-            send(zp.at[rows], zr.at[dy], s_zr.at[dy], r_zr.at[dy], dev(0, 0, dy))
+            send(zp.at[rows], zr.at[dy], s_zr.at[0], r_zr.at[0], dev(0, 0, dy))
 
     def ctx_near():
         ctx_wait(2)
@@ -288,9 +288,9 @@
 
     def ctx_pass():
         ctx_wait(1)
-        ctx_forward(5, -1, 0, 1, 5)
+        ctx_forward(5, -1, 0, 1)
         ctx_wait(4)
-        ctx_forward(6, 1, 1, -1, 6)
+        ctx_forward(6, 1, 1, -1)
 
     def ctx_far():
         ctx_wait(5)
@@ -302,13 +302,16 @@
     def sw(k):
         return lambda: sib_wait(k)
 
-    ctx_second = lambda: ctx_sends_to(1, -lead, jnp.where(c == 0, 3, 2))
+    ctx_second = lambda: ctx_sends_to(-lead, jnp.where(c == 0, 3, 2))
 
     def low_rank_terms():
-        for ys in range(NY):
-            @pl.when(jnp.logical_not(jnp.logical_and(diag, y == ys)))
-            def _():
-                arrived(zall.at[ys], r_zd.at[ys])
+        @pl.when(diag)
+        def _():
+            arrived(first_three(zall), r_zd.at[0])
+
+        @pl.when(off)
+        def _():
+            arrived(zall, r_zd.at[0])
 
         arrived(buT.at[c], r_bu.at[2])
         arrived(gr.at[c], r_bu.at[3])
@@ -352,20 +355,24 @@
 
     def early_send():
         for dx in range(1, NX):
-            send(es.at[0], es.at[dx], s_es.at[dx], r_es.at[dx], (mod4(x + dx), z, y, c))
+            send(es.at[0], es.at[dx], s_es.at[0], r_es.at[0], (mod4(x + dx), z, y, c))
+
+    both = lambda *fs: lambda: [f() for f in fs]
+    idle = lambda: None
 
     hop(1, ctx_second, zp_sum, zp_send)
-    hop(2, sw(0), m((0,), 0), lambda: None)
-    hop(3, sw(1), m((0,), 1), ctx_pass)
-    hop(4, sw(2), m((0,), 2), ctx_near, m((1, 3), 0), m((1, 3), 1), lambda: (low_rank_sum(), resid_half()))
-    hop(5, m((1, 3), 2), sw(3), m((1, 3), 3), m((0,), 3), lambda: None, adapter_on)
-    hop(6, sw(4), m((1, 3), 4), m((0,), 4), second_leg, ctx_far, m((2,), 0))
-    hop(7, m((2,), 1, 2), m((2,), 3), sw(5), m((1, 3), 5), m((0,), 5), m((2,), 4, 5))
-    hop(8, low_rank_terms, sw(6), m((1, 2), 6), m((0, 3), 6), early_sums, early_send)
+    hop(2, sw(0), m((0,), 0), ctx_pass)
+    hop(3, both(sw(1), m((0,), 1)), idle, ctx_near)
+    hop(4, both(sw(2), m((0,), 2), m((1, 3), 0)), both(m((1, 3), 1, 2)), both(low_rank_sum, resid_half, adapter_on))
+    hop(5, both(sw(3), m((0,), 3)), both(m((1, 3), 3), ctx_far), m((2,), 0, 1))
+    hop(6, both(sw(4), m((1, 3), 4)), both(m((0, 2), 4), second_leg), m((2,), 2, 3))
+    hop(7, both(sw(5), m((1, 3), 5)), m((0, 2), 5), low_rank_terms)
+    hop(8, sw(6), m((1, 3), 6), m((0, 2), 6))
     sib_wait(7)
-    mm((0, 1, 2, 3), 7)
-    sib_wait(8)
-    mm((0, 1, 2, 3), 8)
+    mm((1, 3), 7)
+    mm((2, 0), 7)
+    early_sums()
+    early_send()
 
     for cc in range(2):
         @pl.when(jnp.logical_not(jnp.logical_and(diag, c == cc)))
@@ -376,9 +383,10 @@
 
     jown = mod4(y - x)
     for k, (lo, hi) in enumerate(CHUNKS):
-        for dy in range(1, NY):
-            piece = pl.ds(lo * COLS, (hi - lo) * COLS)
-            arrived(rsb.at[mod4(y - dy), piece], r_rs.at[dy, k])
+        if k in (0, NCH - 1):
+            start = lo * COLS
+            rows = pl.ds(start, (CHUNKS[-2][1] if k == 0 else hi) * COLS - start)
+            arrived(rsb.at[pl.ds(0, 3), rows], r_rs.at[k // (NCH - 1)])
         for slot in range(lo, hi):
             step = (slot + 1) // 2
             zz = z if slot == 0 else (z - step if slot % 2 == 1 else z + step)
@@ -402,24 +410,26 @@
         g1, g3 = split2(gh)
         acc = acc + dot(buT[cc], jnp.concatenate([h1, h2, g1, g3], axis=1), TN)
         sums = [s + fold(t) for s, t in zip(sums, (h, h * h, h * d, gh, gh * h, gh * d))]
+    for n, s in enumerate(sums):
+        ts[0, n:n + 1] = jnp.sum(s, axis=0, keepdims=True)
+    ts[0, 6:] = jnp.zeros((2, SEQ), F32)
+    for dx in (2, 1, 3):
+        send(ts.at[0], ts.at[dx], s_ts.at[0], r_ts.at[0], (mod4(x + dx), z, y, c))
     ls[0, 0:RANK] = acc[0:RANK, 0:SEQ] + acc[0:RANK, SEQ:2 * SEQ]
-    ls[0, RANK:2 * RANK] = acc[0:RANK, 2 * SEQ:3 * SEQ] + acc[0:RANK, 3 * SEQ:]
-    for n, s in enumerate(sums):
-        ls[0, 2 * RANK + n:2 * RANK + n + 1] = jnp.sum(s, axis=0, keepdims=True)
-    ls[0, 2 * RANK + 6:] = jnp.zeros((2, SEQ), F32)
+    ls[0, RANK:] = acc[0:RANK, 2 * SEQ:3 * SEQ] + acc[0:RANK, 3 * SEQ:]
+    for dx in (2, 1, 3):
+        send(ls.at[0], ls.at[dx], s_st.at[0], r_st.at[0], (mod4(x + dx), z, y, c))
+    early = es[0]
+    arrived(last_three(es), r_es.at[0])
     for dx in range(1, NX):
-        send(ls.at[0], ls.at[dx], s_st.at[dx], r_st.at[dx], (mod4(x + dx), z, y, c))
-    early = es[0]
+        early = early + es[dx]
+    late = ts[0]
+    arrived(last_three(ts), r_ts.at[0])
     for dx in range(1, NX):
-        arrived(es.at[dx], r_es.at[dx])
-        early = early + es[dx]
-    late = ls[0]
-    for dx in range(1, NX):
-        arrived(ls.at[dx], r_st.at[dx])
-        late = late + ls[dx]
+        late = late + ts[dx]
     inv = 1.0 / WIDTH
     m1, e_gd, e_g = [early[2 * RANK + n:2 * RANK + n + 1] * inv for n in range(3)]
-    mu, e_hh, e_hd, e_gh, e_ghh, e_ghd = [late[2 * RANK + n:2 * RANK + n + 1] * inv for n in range(6)]
+    mu, e_hh, e_hd, e_gh, e_ghh, e_ghd = [late[n:n + 1] * inv for n in range(6)]
     rinv = lax.rsqrt(e_hh - mu * mu + 1e-05)
     m2 = rinv * (e_hd - mu * m1)
     g_n = rinv * (e_gh - mu * e_g)
@@ -428,6 +438,10 @@
     lr = live * rinv
     m3 = lr * (e_gd - m1 * e_g - m2 * g_n)
     m4 = lr * (g_nd - m1 * g_n - m2 * g_nn)
+    late = ls[0]
+    arrived(last_three(ls), r_st.at[0])
+    for dx in range(1, NX):
+        late = late + ls[dx]
     b_one = jnp.broadcast_to(early[RANK:2 * RANK, 0:1], (RANK, SEQ))
     b_g = jnp.broadcast_to(early[RANK:2 * RANK, SEQ - 1:SEQ], (RANK, SEQ))
     b_n = rinv * (late[0:RANK] - mu * b_one)
@@ -436,8 +450,8 @@
     q1, q2 = split2(rinv * (b_c - m3 * b_one - m4 * b_n))
     xq = y
     qg[xq] = jnp.concatenate([q1, q2], axis=0).T
-    for dy in range(1, NY):
-        send(qg.at[xq], qg.at[xq], s_q.at[dy], r_q.at[dy], dev(0, 0, dy))
+    for dy in (2, 1, 3):
+        send(qg.at[xq], qg.at[xq], s_q.at[0], r_q.at[0], dev(0, 0, dy))
 
     z1, z2 = split2(jnp.concatenate([zall[0], zall[1]], axis=0))
     zs = jnp.concatenate([z1, z2], axis=0)
@@ -456,14 +470,13 @@
     for dp in range(NX):
         p = mod4(x + dp)
         me = jnp.logical_and(diag, dp == 0)
-        send_unless(me, hb_red.at[p], hb_rcv.at[y], s_hb.at[dp], r_hb.at[y], (p, z, x, c))
+        send_unless(me, hb_red.at[p], hb_rcv.at[y], s_hb.at[0], r_hb.at[0], (p, z, x, c))
 
     @pl.when(diag)
     def _():
         hb_rcv[y] = hb_red[x]
 
-    for dy in range(1, NY):
-        arrived(qg.at[xq], r_q.at[dy])
+    arrived(first_three(qg), r_q.at[0])
     qs = jnp.concatenate([qg[xb] for xb in range(NX)], axis=0)
     mine = pl.ds(pl.multiple_of(x * 160, 32), 160)
     for cc in range(2):
@@ -477,38 +490,64 @@
     for k in range(5):
         pairs.append(jnp.where(low, ha_sum[pl.ds(2 * k, NZ, stride=10)], ha_sum[pl.ds(2 * k + 1, NZ, stride=10)]))
     v = jnp.concatenate(pairs, axis=1)
+    @pl.when(diag)
+    def _():
+        arrived(first_three(hb_rcv), r_hb.at[0])
+
+    @pl.when(off)
+    def _():
+        arrived(hb_rcv, r_hb.at[0])
+
+    v = jnp.concatenate([v, hb_rcv[0] + hb_rcv[1] + hb_rcv[2] + hb_rcv[3]], axis=1)
     for zi in range(NZ):
-        ha2[zi] = v[zi:zi + 1]
+        ab[zi] = v[zi:zi + 1]
+    for dz in (8, 7, 9, 6, 10, 5, 11, 4, 12, 3, 13, 2, 14, 1, 15):
+        send(ab.at[lax.rem(z + dz, NZ)], abz.at[dz], s_ab.at[0], r_ab.at[0], dev(0, dz))
+    acc = ab[z]
+    arrived(abz.at[pl.ds(1, NZ - 1)], r_ab.at[0])
     for dz in range(1, NZ):
-        send(ha2.at[lax.rem(z + dz, NZ)], haz.at[dz], s_az.at[dz], r_az.at[dz], dev(0, dz))
-    for ys in range(NY):
-        @pl.when(jnp.logical_not(jnp.logical_and(diag, y == ys)))
-        def _():
-            arrived(hb_rcv.at[ys], r_hb.at[ys])
-    acc = hb_rcv[0] + hb_rcv[1] + hb_rcv[2] + hb_rcv[3]
-    for zi in range(NZ):
-        hb2[zi] = acc[zi:zi + 1]
-    for dz in range(1, NZ):
-        send(hb2.at[lax.rem(z + dz, NZ)], hbz.at[dz], s_bz.at[dz], r_bz.at[dz], dev(0, dz))
-    acc = ha2[z]
-    for dz in range(1, NZ):
-        arrived(haz.at[dz], r_az.at[dz])
-        acc = acc + haz[dz]
+        acc = acc + abz[dz]
     for k in range(10):
         out_a[k:k + 1] = acc[:, k * RANK:(k + 1) * RANK]
-    acc = hb2[z]
-    for dz in range(1, NZ):
-        arrived(hbz.at[dz], r_bz.at[dz])
-        acc = acc + hbz[dz]
-    out_b[...] = acc
-
-    for keep, cp in pending:
-        if keep is None:
-            cp.wait_send()
-        else:
-            @pl.when(keep)
-            def _():
-                cp.wait_send()
+    out_b[...] = acc[:, HALF:]
+
+    left(wg.at[c, pl.ds(0, NZ - 1)], s_w.at[0])
+    left(wg.at[c], s_ws.at[0])
+    left(first_three(ctxg), s_ctx.at[0])
+    left(ctxg.at[0, 0], s_ctx.at[1])
+    left(adg.at[c], s_ad.at[0])
+    for half in range(2):
+        @pl.when(jnp.logical_not(jnp.logical_and(diag, c == half)))
+        def _():
+            left(rt.at[half], s_res.at[half])
+
+    @pl.when(jnp.logical_and(diag, c == 0))
+    def _():
+        left(first_three(relay), s_rel.at[0])
+
+    left(buT.at[c], s_bu.at[2])
+    left(gr.at[c], s_bu.at[3])
+    left(first_three(part), s_rs.at[0])
+    left(first_three(zr), s_zr.at[0])
+    left(first_three(es), s_es.at[0])
+    left(first_three(ts), s_ts.at[0])
+    left(first_three(ls), s_st.at[0])
+    left(first_three(qg), s_q.at[0])
+    left(hb_sib, s_hs.at[0])
+    left(ha_sib, s_ha.at[0])
+    left(ab.at[pl.ds(0, NZ - 1)], s_ab.at[0])
+
+    @pl.when(diag)
+    def _():
+        left(ctxg.at[pl.ds(0, 3), 0], s_bu.at[0])
+        left(first_three(ts), s_bu.at[1])
+        left(first_three(zall), s_zd.at[0])
+        left(first_three(hb_red), s_hb.at[0])
+
+    @pl.when(off)
+    def _():
+        left(zall, s_zd.at[0])
+        left(hb_red, s_hb.at[0])
 
 
 def body(ctx, resid, w, a, b, d, u, gain, lengths):
@@ -541,7 +580,8 @@
             pltpu.VMEM((32, SEQ), F32),
             pltpu.VMEM((NY, 32, SEQ), F32),
             pltpu.VMEM((NX, 2 * RANK + 8, SEQ), F32),
-            pltpu.VMEM((NX, 2 * RANK + 8, SEQ), F32),
+            pltpu.VMEM((NX, 8, SEQ), F32),
+            pltpu.VMEM((NX, 2 * RANK, SEQ), F32),
             pltpu.VMEM((FEATS, SEQ), F32),
             pltpu.VMEM((FEATS, SEQ), F32),
             pltpu.VMEM((FEATS, SEQ), F32),
@@ -553,16 +593,12 @@
             pltpu.VMEM((NX, 16, HALF), F32),
             pltpu.VMEM((NY, 16, HALF), F32),
             pltpu.VMEM((160, SEQ), F32),
-            pltpu.VMEM((NZ, 1, HALF), F32),
-            pltpu.VMEM((NZ, 1, HALF), F32),
-            pltpu.VMEM((NZ, 1, HALF), F32),
-            pltpu.VMEM((NZ, 1, HALF), F32),
-            dma(9),
-            dma(7), dma(7), dma(16 * NP), dma(16 * NP), dma(16), dma(16), dma(1), dma(1), dma(2), dma(NX, 2), dma(NX, 2), dma(2),
-            dma(8), dma(4), dma(NX, NCH), dma(NY, NCH),
-            dma(NY), dma(NY), dma(NX), dma(NY), dma(NX), dma(NX), dma(NX), dma(NX), dma(NY), dma(NY), dma(1), dma(1),
-            dma(1), dma(1),
-            dma(NX), dma(NY), dma(NZ), dma(NZ), dma(NZ), dma(NZ),
+            pltpu.VMEM((NZ, 1, 2 * HALF), F32),
+            pltpu.VMEM((NZ, 1, 2 * HALF), F32),
+            dma(9), dma(2), dma(7), dma(1), dma(8 * NP), dma(1), dma(NCH), dma(1), dma(1), dma(2), dma(1), dma(1), dma(2),
+            dma(4), dma(4), dma(1), dma(2),
+            dma(1), dma(1), dma(1), dma(1), dma(1), dma(1), dma(1), dma(1), dma(1), dma(1), dma(1), dma(1),
+            dma(1), dma(1), dma(1), dma(1), dma(1), dma(1), dma(1), dma(1),
         ],
         compiler_params=pltpu.CompilerParams(collective_id=0, has_side_effects=True, vmem_limit_bytes=60 << 20),
         cost_estimate=pl.CostEstimate(flops=2 * 1280 * 1280 * 512, bytes_accessed=2 << 20, transcendentals=0),

time: 78.5 us -> 73.8 us (0.940)
  Pallas kernels: 75.2 us -> 71.1 us
    pallas_call x1, Pallas kernels: 75.2 us -> 71.1 us  [body(): pl.pallas_call(kernel, out_shape=(jax.ShapeDtypeStruct((10, RANK), F32),...]
where the time goes in v4:
time: 73.8 us; the launch traced here: 73.6 us
  Pallas kernels  71.1 us (96%)
  local copies, waits for them, and re-layouts  1.88 us (3%)
    pallas_call x1, Pallas kernels, body(): pl.pallas_call(kernel, out_shape=(jax.ShapeDtypeStruct((10, RANK), F32),...  71.1 us
    unnamed x4, local copies, waits for them, and re-layouts  1.88 us

profile of v4, /device:TPU:1, one launch (start us, length us, event | category | flops | bytes accessed | tf_op | source)
XLA Modules:
  0.0 73.6 jit_solution(17850658199154729559)
XLA Ops:
  0.6 71.1 %hvp.1 = (f32[10,64]{1,0:T(8,128)}, f32[1,640]{1,0:T(1,128)}) custom-call(bf16[256,640]{1,0:T(8,128)(2,1)} %ctx_ref.1, bf16[256,640]{1,0:T(8,128)(2,1)} %resid_ref.1, bf16[80,640]{1,0:T(8,128)(2,1)} %bitcast.4, bf16[64,640]{1,0:T(8,128)(2,1)} %bitcast.5, bf16[64,640]{1,0:T(8,128)(2,1)} %bitcast.6, bf16[64,640]{1,0:T(8,128)(2,1)} %b_ref.1, ...), custom_call_target="tpu_custom_call" | custom-call | flops 1677721600 | bytes 2097152 | tf_op jit(solution)/shard_map/hvp/pallas_call | solution.py:556
  71.8 0.0 copy-start
  71.8 1.3 %copy.13 = f32[10,64]{1,0:T(8,128)} copy(f32[10,64]{1,0:T(8,128)} %get-tuple-element.4) | data formatting | bytes 5120
  73.1 0.0 copy-done
  73.1 0.6 copy.14
Async XLA Ops:
  71.8 1.3 %copy-start = (f32[1,640]{1,0:T(1,128)S(1)}, f32[1,640]{1,0:T(1,128)}, u32[]{:S(2)}) copy-start(f32[1,640]{1,0:T(1,128)} %get-tuple-element.5) | copy-start | bytes 7684

commit v5 on v4

--- a/solution.py
+++ b/solution.py
@@ -361,16 +361,15 @@
     idle = lambda: None
 
     hop(1, ctx_second, zp_sum, zp_send)
-    hop(2, sw(0), m((0,), 0), ctx_pass)
+    hop(2, sw(0), m((0,), 0), both(ctx_pass, low_rank_sum, resid_half))
     hop(3, both(sw(1), m((0,), 1)), idle, ctx_near)
-    hop(4, both(sw(2), m((0,), 2), m((1, 3), 0)), both(m((1, 3), 1, 2)), both(low_rank_sum, resid_half, adapter_on))
+    hop(4, both(sw(2), m((0,), 2), m((1, 3), 0)), both(m((1, 3), 1, 2)), adapter_on)
     hop(5, both(sw(3), m((0,), 3)), both(m((1, 3), 3), ctx_far), m((2,), 0, 1))
     hop(6, both(sw(4), m((1, 3), 4)), both(m((0, 2), 4), second_leg), m((2,), 2, 3))
     hop(7, both(sw(5), m((1, 3), 5)), m((0, 2), 5), low_rank_terms)
     hop(8, sw(6), m((1, 3), 6), m((0, 2), 6))
     sib_wait(7)
-    mm((1, 3), 7)
-    mm((2, 0), 7)
+    mm((0, 1, 2, 3), 7)
     early_sums()
     early_send()
 

time: 73.8 us -> 73.2 us (level); the launches traced: 73.6 us -> 71.9 us
  Pallas kernels: 71.1 us -> 69.4 us
    pallas_call x1, Pallas kernels: 71.1 us -> 69.4 us  [body(): pl.pallas_call(kernel, out_shape=(jax.ShapeDtypeStruct((10, RANK), F32),...]
where the time goes in v5:
time: 73.2 us; the launch traced here: 71.9 us
  Pallas kernels  69.4 us (95%)
  local copies, waits for them, and re-layouts  1.88 us (3%)
    pallas_call x1, Pallas kernels, body(): pl.pallas_call(kernel, out_shape=(jax.ShapeDtypeStruct((10, RANK), F32),...  69.4 us
    unnamed x4, local copies, waits for them, and re-layouts  1.88 us

profile of v5, /device:TPU:1, one launch (start us, length us, event | category | flops | bytes accessed | tf_op | source)
XLA Modules:
  0.0 71.9 jit_solution(9785708623921129682)
XLA Ops:
  0.6 69.4 %hvp.1 = (f32[10,64]{1,0:T(8,128)}, f32[1,640]{1,0:T(1,128)}) custom-call(bf16[256,640]{1,0:T(8,128)(2,1)} %ctx_ref.1, bf16[256,640]{1,0:T(8,128)(2,1)} %resid_ref.1, bf16[80,640]{1,0:T(8,128)(2,1)} %bitcast.4, bf16[64,640]{1,0:T(8,128)(2,1)} %bitcast.5, bf16[64,640]{1,0:T(8,128)(2,1)} %bitcast.6, bf16[64,640]{1,0:T(8,128)(2,1)} %b_ref.1, ...), custom_call_target="tpu_custom_call" | custom-call | flops 1677721600 | bytes 2097152 | tf_op jit(solution)/shard_map/hvp/pallas_call | solution.py:555
  70.0 0.0 copy-start
  70.0 1.3 %copy.13 = f32[10,64]{1,0:T(8,128)} copy(f32[10,64]{1,0:T(8,128)} %get-tuple-element.4) | data formatting | bytes 5120
  71.3 0.0 copy-done
  71.3 0.6 copy.14
Async XLA Ops:
  70.0 1.3 %copy-start = (f32[1,640]{1,0:T(1,128)S(1)}, f32[1,640]{1,0:T(1,128)}, u32[]{:S(2)}) copy-start(f32[1,640]{1,0:T(1,128)} %get-tuple-element.5) | copy-start | bytes 7684

commit v6 on v5

--- a/solution.py
+++ b/solution.py
@@ -366,10 +366,13 @@
     hop(4, both(sw(2), m((0,), 2), m((1, 3), 0)), both(m((1, 3), 1, 2)), adapter_on)
     hop(5, both(sw(3), m((0,), 3)), both(m((1, 3), 3), ctx_far), m((2,), 0, 1))
     hop(6, both(sw(4), m((1, 3), 4)), both(m((0, 2), 4), second_leg), m((2,), 2, 3))
-    hop(7, both(sw(5), m((1, 3), 5)), m((0, 2), 5), low_rank_terms)
-    hop(8, sw(6), m((1, 3), 6), m((0, 2), 6))
+    hop(7, both(sw(5), m((1, 3), 5)), m((0, 2), 5), idle)
+    hop(8)
+    sib_wait(6)
+    mm((0, 1, 2, 3), 6)
     sib_wait(7)
     mm((0, 1, 2, 3), 7)
+    low_rank_terms()
     early_sums()
     early_send()
 

time: 73.2 us -> 72.9 us (level)
  the two profiles are of different devices: /device:TPU:1 before, /device:TPU:3 now
where the time goes in v6:
time: 72.9 us; the launch traced here: 72.8 us
  Pallas kernels  70.2 us (96%)
  local copies, waits for them, and re-layouts  1.88 us (3%)
    pallas_call x1, Pallas kernels, body(): pl.pallas_call(kernel, out_shape=(jax.ShapeDtypeStruct((10, RANK), F32),...  70.2 us
    unnamed x4, local copies, waits for them, and re-layouts  1.88 us

profile of v6, /device:TPU:3, one launch (start us, length us, event | category | flops | bytes accessed | tf_op | source)
XLA Modules:
  0.0 72.8 jit_solution(17296217137596199788)
XLA Ops:
  0.6 70.2 %hvp.1 = (f32[10,64]{1,0:T(8,128)}, f32[1,640]{1,0:T(1,128)}) custom-call(bf16[256,640]{1,0:T(8,128)(2,1)} %ctx_ref.1, bf16[256,640]{1,0:T(8,128)(2,1)} %resid_ref.1, bf16[80,640]{1,0:T(8,128)(2,1)} %bitcast.4, bf16[64,640]{1,0:T(8,128)(2,1)} %bitcast.5, bf16[64,640]{1,0:T(8,128)(2,1)} %bitcast.6, bf16[64,640]{1,0:T(8,128)(2,1)} %b_ref.1, ...), custom_call_target="tpu_custom_call" | custom-call | flops 1677721600 | bytes 2097152 | tf_op jit(solution)/shard_map/hvp/pallas_call | solution.py:558
  70.9 0.0 copy-start
  70.9 1.3 %copy.13 = f32[10,64]{1,0:T(8,128)} copy(f32[10,64]{1,0:T(8,128)} %get-tuple-element.4) | data formatting | bytes 5120
  72.2 0.0 copy-done
  72.2 0.6 copy.14
Async XLA Ops:
  70.9 1.3 %copy-start = (f32[1,640]{1,0:T(1,128)S(1)}, f32[1,640]{1,0:T(1,128)}, u32[]{:S(2)}) copy-start(f32[1,640]{1,0:T(1,128)} %get-tuple-element.5) | copy-start | bytes 7684
